TPU v7x, 32 devices: a whole 2x2x4 slice. The times are simulated.
32 devices in a mesh: tube: 2 (over x), gy: 4 (over y, core), gz: 4 (over z).
Axes of the slice: x: 2, y: 2, z: 4, core: 2. Of those that a mesh axis runs over, the one named last changes fastest.
Arguments:
- state: float32 [13, 32, 32, 512], P(None, 'tube', 'gy', 'gz'), as said below
- fresh: float32 [13, 32, 512], P(None, 'gy', 'gz'), as said below
- substeps: int32 [32, 32, 512], P('tube', 'gy', 'gz'), may hold values from 1 to 8, as said below
- shift: int32 [], replicated, may hold values from 1 to 12
Outputs:
- advanced: float32 [13, 32, 32, 512], P(None, 'tube', 'gy', 'gz')
Inputs may be any that keep to these rules, and one draw needn't show every extreme that they name: `state`: the first nine components are positive partial densities; the energy exceeds the kinetic and chemical energy by a positive thermal part. `fresh`: the same conventions as state. `substeps`: at most 8; some cell takes 8 in every draw.
All inputs are finite; a program needn't handle non-finite values.
Results may differ from a plain program's by a relative error of at most 0.0003.
Values sent between devices are 32-bit elements; how exact they have to be, the bound alone decides.
No kernel may reach another device: no remote copies, remote signals or barrier semaphores. Data moves between devices by JAX's collectives and lax.ppermute only.
A program may use at most 64 MiB of HBM per device.

v0:
```python
import functools

import jax
import jax.numpy as jnp
import numpy as np
from jax import lax
from jax.experimental import pallas as pl
from jax.experimental.pallas import tpu as pltpu
from jax.sharding import PartitionSpec as P

SMAX = 12
HALO = 3
NCOMP = 13
ROWS = 8
SCALE = 0.25
TIME_STEP = 0.05
FLUX_FACTOR = -TIME_STEP / (6.0 * SCALE)

MOLAR = np.array([2.016, 31.998, 18.015, 1.008, 15.999, 17.007, 33.006, 34.014, 28.014]) / 18.015
GAS = 1.0 / MOLAR
FORMATION = np.array([0.0, 0.0, -1.5, 12.0, 1.5, 0.25, 0.02, -0.45, 0.0])
REACTANTS = [
    (3, 1), (4, 5), (4, 0), (3, 5), (0, 5), (2, 3), (4, 2), (5, 5), (0, 8), (3, 3, 8), (4, 4, 8),
    (3, 4, 8), (3, 5, 8), (3, 1, 8), (6, 3), (6, 3), (6, 4), (6, 5), (6, 6), (7, 8), (7, 3),
]
PRODUCTS = [
    (4, 5), (3, 1), (3, 5), (4, 0), (2, 3), (0, 5), (5, 5), (4, 2), (3, 3), (0,), (1,),
    (5,), (2,), (6,), (0, 1), (5, 5), (1, 5), (2, 1), (7, 1), (5, 5), (2, 5),
]
PREFACTOR = [
    30.0, 8.0, 20.0, 6.0, 25.0, 10.0, 12.0, 5.0, 4.0, 20.0, 15.0,
    18.0, 22.0, 25.0, 30.0, 25.0, 20.0, 30.0, 10.0, 6.0, 15.0,
]
BARRIER = [
    4.0, 1.0, 3.0, 1.5, 1.5, 4.5, 4.0, 1.5, 6.0, 0.5, 0.5,
    0.5, 0.5, 0.3, 0.8, 0.5, 0.3, 0.3, 0.5, 5.0, 1.5,
]

KAPPA = 0.609375
EPS = 3.0 * SCALE * SCALE * 1e-6


def rcp(x):
    return pl.reciprocal(x, approx=True)


def correction(d1, d2, d3, d4):
    k2 = KAPPA * (d2 * d2) + EPS
    k3 = KAPPA * (d3 * d3) + EPS
    xa = d1 - 1.375 * d2
    xb = d3 - 0.625 * d2
    xc = d4 - 1.375 * d3
    ra = rcp(xa * xa + k2)
    rb = rcp(xb * xb + k2)
    rc = rcp(xc * xc + k3)
    wa = ra * ra
    wb = 6.0 * (rb * rb)
    wc = 3.0 * (rc * rc)
    return ((xa + xb) * wa + (0.5 * (d2 + d4) - d3) * wc) * rcp(wa + wb + wc)


def face_flux(du, df, f2, f3, alpha):
    e = [alpha * d for d in du]
    p = [df[k] + e[k] for k in range(4)]
    m = [None] + [df[k] - e[k] for k in range(1, 5)]
    linear = 3.0 * (f2 + f3) - e[2] + 0.5 * (p[1] - m[3])
    return linear - correction(p[0], p[1], p[2], p[3]) + correction(m[4], m[3], m[2], m[1])


def sweep(cells, fluxes, alpha, first, last):
    du, df = {}, {}
    out = {}
    for j in range(first, last + 1):
        for k in range(j, j + 5):
            if k not in du:
                du[k] = cells(k + 1) - cells(k)
                df[k] = fluxes(k + 1) - fluxes(k)
        out[j] = face_flux(
            [du[k] for k in range(j, j + 5)],
            [df[k] for k in range(j, j + 5)],
            fluxes(j + 2),
            fluxes(j + 3),
            alpha(j),
        )
    return out


def memo(load):
    return functools.lru_cache(maxsize=None)(load)


def thermo(u):
    g = [u[k] if GAS[k] == 1.0 else u[k] * float(GAS[k]) for k in range(9)]
    s2 = g[2] + g[6] + g[7]
    s3 = g[3] + g[4]
    gas = (g[0] + g[1]) + (g[5] + g[8]) + (s2 + s3)
    heat = 2.5 * gas + (0.5 * s2 - s3)
    bond = 1.5 * (u[4] - u[2]) + 12.0 * u[3] + 0.25 * u[5] + 0.02 * u[6] - 0.45 * u[7]
    rho = ((u[0] + u[1]) + (u[2] + u[3])) + ((u[4] + u[5]) + (u[6] + u[7])) + u[8]
    back = 1.0 / rho
    cold = 1.0 / heat
    motion = 0.5 * (u[9] * u[9] + u[10] * u[10] + u[11] * u[11]) * back
    temperature = (u[12] - motion - bond) * cold
    pressure = gas * temperature
    sound = jnp.sqrt((1.0 + gas * cold) * pressure * back)
    return back, pressure, sound


def for_components(dim, body):
    special = 8 + dim

    def step(i, _):
        body(i + jnp.where(i >= special, 1, 0).astype(jnp.int32), 0)
        return 0

    lax.fori_loop(0, NCOMP - 2, step, 0)
    body(special, 1)
    body(NCOMP - 1, 2)


def flux_of(u, speed, pressure, kind):
    if kind == 0:
        return u * speed
    if kind == 1:
        return u * speed + SCALE * pressure()
    return (u + pressure()) * speed


def alphas(speed, faces, alpha_ref, rows):
    values = memo(lambda i: speed[pl.ds(i * rows, ROWS), :])
    for j in range(faces):
        top = values(j)
        for k in range(1, 6):
            top = jnp.maximum(top, values(j + k))
        alpha_ref[pl.ds(j * rows, ROWS), :] = top


def stage_kernel(
    stage, planes, width_y, width_z, x_msgs, place,
    u_ref, uz_ref, start_ref, fresh_ref, xlo_ref, xhi_ref, ylo_ref, yhi_ref, zlo_ref, zhi_ref,
    *refs,
):
    groups = planes // ROWS
    zvecs = width_z // ROWS
    tubes = place[1]
    tube = place[0]
    first = stage == 1
    last = stage == 3
    refs = list(refs)
    new_ref = refs.pop(0)
    if not last:
        newz_ref = refs.pop(0)
        xmsg_refs = [refs.pop(0) for _ in range(x_msgs)]
        ymsg_lo, ymsg_hi, zmsg_lo, zmsg_hi = [refs.pop(0) for _ in range(4)]
    (
        xh, ux, px, ax, alx, uy, py, ay, aly, uz, pz, az, alz, tmp, accx, accy, accz,
    ) = refs

    def ghosts(c, _):
        for k in range(HALO):
            here = pl.ds(k * ROWS, ROWS)
            lo, hi = xlo_ref[c, here, :], xhi_ref[c, here, :]
            if not first:
                lo = jnp.where(tube == 0, u_ref[c, pl.ds(0, ROWS), :], lo)
                hi = jnp.where(tube == tubes - 1, fresh_ref[c], hi)
            xh[c, here, :] = lo
            xh[c, pl.ds((HALO + k) * ROWS, ROWS), :] = hi
        return 0

    lax.fori_loop(0, NCOMP, ghosts, 0)

    def own(i, _):
        for k in range(2):
            p = i * 2 + k
            here = pl.ds(pl.multiple_of(p * ROWS, ROWS), ROWS)
            u = [u_ref[c, here, :] for c in range(NCOMP)]
            back, pressure, sound = thermo(u)
            back, sound = SCALE * back, SCALE * sound
            there = pl.ds(pl.multiple_of((p + HALO) * ROWS, ROWS), ROWS)
            speeds = [u[9 + d] * back for d in range(3)]
            ux[there, :] = speeds[0]
            px[there, :] = pressure
            ax[there, :] = jnp.abs(speeds[0]) + sound
            ystart = pl.ds(HALO * planes + p, width_y, stride=planes)
            uy[ystart, :] = speeds[1]
            py[ystart, :] = pressure
            ay[ystart, :] = jnp.abs(speeds[1]) + sound
            tmp[0, here, :] = speeds[2]
            tmp[1, here, :] = pressure
            tmp[2, here, :] = jnp.abs(speeds[2]) + sound
        return 0

    lax.fori_loop(0, planes // 2, own, 0)
    for ref, k in ((uz, 0), (pz, 1), (az, 2)):
        ref[pl.ds(ROWS, width_z), :] = tmp[k].T

    def ghost_thermo(u, d, speed_ref, pressure_ref, top_ref, row):
        back, pressure, sound = thermo(u)
        speed = u[9 + d] * (SCALE * back)
        speed_ref[pl.ds(row, ROWS), :] = speed
        pressure_ref[pl.ds(row, ROWS), :] = pressure
        top_ref[pl.ds(row, ROWS), :] = jnp.abs(speed) + SCALE * sound

    for k in range(2 * HALO):
        row = k if k < HALO else planes + k
        u = [xh[c, pl.ds(k * ROWS, ROWS), :] for c in range(NCOMP)]
        ghost_thermo(u, 0, ux, px, ax, row * ROWS)
    for ref, offset in ((ylo_ref, 0), (yhi_ref, HALO + width_y)):
        def ghost_y(k, _, ref=ref, offset=offset):
            for g in range(groups):
                u = [ref[c, pl.ds(k * planes + g * ROWS, ROWS), :] for c in range(NCOMP)]
                ghost_thermo(u, 1, uy, py, ay, (offset + k) * planes + g * ROWS)
            return 0
        lax.fori_loop(0, HALO, ghost_y, 0)
    for ref, row in ((zlo_ref, 0), (zhi_ref, ROWS + width_z)):
        u = [ref[c] for c in range(NCOMP)]
        ghost_thermo(u, 2, uz, pz, az, row)

    alphas(ax, planes + 1, alx, ROWS)
    for g in range(groups):
        values = memo(lambda i: ay[pl.ds(i * planes + g * ROWS, ROWS), :])
        for j in range(width_y + 1):
            top = values(j)
            for k in range(1, 6):
                top = jnp.maximum(top, values(j + k))
            aly[pl.ds(j * planes + g * ROWS, ROWS), :] = top

    def zvec(ref, i):
        return ref[pl.ds(ROWS - HALO + i, ROWS, stride=zvecs), :]

    values_z = memo(lambda i: zvec(az, i))
    for j in range(zvecs + 1):
        top = values_z(j)
        for k in range(1, 6):
            top = jnp.maximum(top, values_z(j + k))
        alz[pl.ds(j * ROWS, ROWS), :] = top

    def x_body(c, kind):
        def cell(i):
            if HALO <= i < planes + HALO:
                return u_ref[c, pl.ds((i - HALO) * ROWS, ROWS), :]
            k = i if i < HALO else i - planes
            return xh[c, pl.ds(k * ROWS, ROWS), :]
        cells = memo(cell)
        fluxes = memo(lambda i: flux_of(
            cells(i), ux[pl.ds(i * ROWS, ROWS), :], lambda: px[pl.ds(i * ROWS, ROWS), :], kind))
        out = sweep(cells, fluxes, lambda j: alx[pl.ds(j * ROWS, ROWS), :], 0, planes)
        for i in range(planes):
            accx[c, pl.ds(i * ROWS, ROWS), :] = out[i + 1] - out[i]

    for_components(1, x_body)

    def y_body(c, kind):
        for g in range(groups):
            def cell(i):
                if HALO <= i < width_y + HALO:
                    return u_ref[c, pl.ds(g * ROWS * width_y + i - HALO, ROWS, stride=width_y), :]
                if i < HALO:
                    return ylo_ref[c, pl.ds(i * planes + g * ROWS, ROWS), :]
                return yhi_ref[c, pl.ds((i - HALO - width_y) * planes + g * ROWS, ROWS), :]
            cells = memo(cell)
            def at(ref):
                return lambda i: ref[pl.ds(i * planes + g * ROWS, ROWS), :]
            fluxes = memo(lambda i: flux_of(cells(i), at(uy)(i), lambda: at(py)(i), kind))
            out = sweep(cells, fluxes, at(aly), 0, width_y)
            for i in range(width_y):
                accy[c, pl.ds(g * ROWS * width_y + i, ROWS, stride=width_y), :] = out[i + 1] - out[i]

    for_components(2, y_body)

    row = lax.broadcasted_iota(jnp.int32, (ROWS, planes * width_y), 0)

    def z_body(c, kind):
        def cell(i):
            value = uz_ref[c, pl.ds(ROWS - HALO + i, ROWS, stride=zvecs), :]
            if i < HALO:
                edge = zlo_ref[c, pl.ds(ROWS - HALO + i, 1), :]
                value = jnp.where(row == 0, edge, value)
            elif i >= zvecs + HALO:
                edge = zhi_ref[c, pl.ds(i - zvecs - HALO, 1), :]
                value = jnp.where(row == ROWS - 1, edge, value)
            return value
        cells = memo(cell)
        fluxes = memo(lambda i: flux_of(cells(i), zvec(uz, i), lambda: zvec(pz, i), kind))
        out = sweep(cells, fluxes, lambda j: alz[pl.ds(j * ROWS, ROWS), :], 0, zvecs)
        for i in range(zvecs):
            accz[c, pl.ds(i, ROWS, stride=zvecs), :] = out[i + 1] - out[i]

    for_components(3, z_body)

    def combine(c, _):
        change = FLUX_FACTOR * (accz[c].T + accx[c] + accy[c])
        if stage == 1:
            value = u_ref[c] + change
        elif stage == 2:
            value = 0.75 * start_ref[c] + 0.25 * (u_ref[c] + change)
        else:
            value = (1.0 / 3.0) * start_ref[c] + (2.0 / 3.0) * (u_ref[c] + change)
        new_ref[c] = value
        if not last:
            newz_ref[c, pl.ds(ROWS, width_z), :] = value.T
        return 0

    lax.fori_loop(0, NCOMP, combine, 0)
    if not last:
        messages(planes, width_y, width_z, place, new_ref, newz_ref, xmsg_refs,
                 ymsg_lo, ymsg_hi, zmsg_lo, zmsg_hi)


def messages(planes, width_y, width_z, place, u_ref, uz_ref, xmsg_refs, ylo, yhi, zlo, zhi):
    def body(c, _):
        for n, ref in enumerate(xmsg_refs):
            begin = place[2 + n]
            for k in range(HALO):
                rows = pl.ds(pl.multiple_of((begin + k) * ROWS, ROWS), ROWS)
                ref[c, pl.ds(k * ROWS, ROWS), :] = u_ref[c, rows, :]
        for k in range(HALO):
            for g in range(planes // ROWS):
                there = pl.ds(k * planes + g * ROWS, ROWS)
                base = g * ROWS * width_y + k
                yhi[c, there, :] = u_ref[c, pl.ds(base, ROWS, stride=width_y), :]
                ylo[c, there, :] = u_ref[
                    c, pl.ds(base + width_y - HALO, ROWS, stride=width_y), :]
        zhi[c] = uz_ref[c, pl.ds(ROWS, ROWS), :]
        zlo[c] = uz_ref[c, pl.ds(width_z, ROWS), :]
        return 0

    lax.fori_loop(0, NCOMP, body, 0)


def assemble_kernel(
    planes, width_y, width_z, place, state_ref, ahead_ref, behind_ref, fresh_ref,
    u_ref, uz_ref, xlo_ref, xhi_ref, ymsg_lo, ymsg_hi, zmsg_lo, zmsg_hi, joined,
):
    tube, tubes, shift = place[0], place[1], place[4]
    tail = behind_ref.shape[1] // ROWS
    total = tail + planes + ahead_ref.shape[1] // ROWS

    def body(c, _):
        joined[pl.ds(0, tail * ROWS), :] = behind_ref[c]
        joined[pl.ds(tail * ROWS, planes * ROWS), :] = state_ref[c]
        fresh = fresh_ref[c]
        for i in range(tail + planes, total):
            value = ahead_ref[c, pl.ds((i - tail - planes) * ROWS, ROWS), :]
            joined[pl.ds(i * ROWS, ROWS), :] = jnp.where(tube == tubes - 1, fresh, value)

        def plane(i):
            return joined[pl.ds(pl.multiple_of((tail + shift + i) * ROWS, ROWS), ROWS), :]

        for i in range(planes):
            u_ref[c, pl.ds(i * ROWS, ROWS), :] = plane(i)
        ground = plane(0)
        for k in range(HALO):
            xhi_ref[c, pl.ds(k * ROWS, ROWS), :] = plane(planes + k)
            xlo_ref[c, pl.ds(k * ROWS, ROWS), :] = jnp.where(tube == 0, ground, plane(k - HALO))
        uz_ref[c, pl.ds(ROWS, width_z), :] = u_ref[c].T
        return 0

    lax.fori_loop(0, NCOMP, body, 0)
    messages(planes, width_y, width_z, place, u_ref, uz_ref, [],
             ymsg_lo, ymsg_hi, zmsg_lo, zmsg_hi)


def powers_of(back):
    a = jnp.exp(-0.5 * back)
    b = jnp.exp(-0.3 * back)
    a2 = a * a
    a3 = a2 * a
    a4 = a2 * a2
    a6 = a3 * a3
    a8 = a4 * a4
    return {0.5: a, 0.3: b, 1.0: a2, 1.5: a3, 3.0: a6, 4.0: a8, 4.5: a8 * a, 5.0: a8 * a2,
            6.0: a6 * a6, 0.8: a * b}


def react(conc, internal, size):
    s2 = conc[2] + conc[6] + conc[7]
    s3 = conc[3] + conc[4]
    heat = 2.5 * (((conc[0] + conc[1]) + (conc[5] + conc[8])) + (s2 + s3)) + (0.5 * s2 - s3)
    bond = None
    for k in range(9):
        if FORMATION[k]:
            term = float(FORMATION[k] * MOLAR[k]) * conc[k]
            bond = term if bond is None else bond + term
    boltzmann = powers_of(heat / (internal - bond))
    pairs = {}
    omega = [None] * 9

    def add(k, value):
        omega[k] = value if omega[k] is None else omega[k] + value

    def sub(k, value):
        omega[k] = -value if omega[k] is None else omega[k] - value

    def rate(j):
        names = REACTANTS[j]
        key = tuple(sorted(names))
        if key not in pairs:
            value = conc[names[0]] * conc[names[1]]
            if len(names) == 3:
                base = tuple(sorted(names[:2]))
                if base not in pairs:
                    pairs[base] = value
                value = pairs[base] * conc[8]
            pairs[key] = value
        return (PREFACTOR[j] * boltzmann[BARRIER[j]]) * pairs[key]

    j = 0
    while j < len(REACTANTS):
        value = rate(j)
        back = j + 1 < len(REACTANTS) and REACTANTS[j + 1] == PRODUCTS[j] \
            and PRODUCTS[j + 1] == REACTANTS[j]
        if back:
            value = value - rate(j + 1)
        for k in range(9):
            times = PRODUCTS[j].count(k) - REACTANTS[j].count(k)
            if times == 0:
                continue
            amount = value if abs(times) == 1 else value + value
            if times > 0:
                add(k, amount)
            else:
                sub(k, amount)
        j += 2 if back else 1
    return [conc[k] + size * omega[k] for k in range(9)]


def chemistry_kernel(planes, span, third_ref, counts_ref, out_ref):
    for c in range(9, NCOMP):
        out_ref[c] = third_ref[c]

    def block(i, _):
        rows = [
            pl.ds(pl.multiple_of((i * span + k) * ROWS, ROWS), ROWS) for k in range(span)
        ]
        counts = [counts_ref[r, :] for r in rows]
        sizes = [TIME_STEP / n.astype(jnp.float32) for n in counts]
        most = counts[0]
        for n in counts[1:]:
            most = jnp.maximum(most, n)
        turns = jnp.max(most)
        conc, internal = [], []
        for r in rows:
            u = [third_ref[c, r, :] for c in range(NCOMP)]
            rho = ((u[0] + u[1]) + (u[2] + u[3])) + ((u[4] + u[5]) + (u[6] + u[7])) + u[8]
            internal.append(
                u[12] - 0.5 * (u[9] * u[9] + u[10] * u[10] + u[11] * u[11]) / rho)
            conc.append([u[k] * float(GAS[k]) for k in range(9)])

        def advance(index, carry):
            new = []
            for k in range(span):
                moved = react(carry[k], internal[k], sizes[k])
                keep = index < counts[k]
                new.append([jnp.where(keep, m, o) for m, o in zip(moved, carry[k])])
            return new

        conc = lax.fori_loop(0, turns, advance, conc)
        for k in range(span):
            for c in range(9):
                out_ref[c, rows[k], :] = conc[k][c] * float(MOLAR[c])
        return 0

    lax.fori_loop(0, planes // span, block, 0)


def shape(*dims):
    return jax.ShapeDtypeStruct(dims, jnp.float32)


def call(kernel, out_shape, scratch, n_in):
    vmem = pl.BlockSpec(memory_space=pltpu.VMEM)
    return pl.pallas_call(
        kernel,
        out_shape=out_shape,
        in_specs=[pl.BlockSpec(memory_space=pltpu.SMEM)] + [vmem] * (n_in - 1),
        out_specs=jax.tree.map(lambda _: vmem, out_shape),
        scratch_shapes=scratch,
        compiler_params=pltpu.CompilerParams(vmem_limit_bytes=48 * 1024 * 1024),
    )


def moved(value, axis, steps, closed):
    count = lax.axis_size(axis)
    pairs = [(i, (i + steps) % count) for i in range(count) if closed or 0 <= i + steps < count]
    return lax.ppermute(value, axis, pairs)


def on_device(state, fresh, substeps, shift):
    comps, planes, width_y, width_z = state.shape
    cross = planes * width_y
    tubes = lax.axis_size("tube")
    tube = lax.axis_index("tube")
    swap = tubes == 2
    x_msgs = 1 if swap else 2
    begins = [jnp.where(tube == 0, planes - HALO, 0), 0] if swap else [0, planes - HALO]
    place = jnp.stack([
        tube.astype(jnp.int32), jnp.int32(tubes), jnp.asarray(begins[0], jnp.int32),
        jnp.asarray(begins[1], jnp.int32), shift.astype(jnp.int32)])

    reach = SMAX + HALO
    flat = state.reshape(comps, cross, width_z)
    if swap:
        out = jnp.where(tube == 0, flat[:, cross - reach * width_y:], flat[:, :reach * width_y])
        ahead = lax.ppermute(out, "tube", [(0, 1), (1, 0)])
        behind = ahead[:, (reach - 2) * width_y:]
    else:
        ahead = moved(flat[:, :reach * width_y], "tube", -1, False)
        behind = moved(flat[:, cross - 2 * width_y:], "tube", 1, False)

    full = shape(comps, cross, width_z)
    fullz = shape(comps, width_z + 2 * ROWS, cross)
    xs = shape(comps, HALO * ROWS, width_z)
    ys = shape(comps, HALO * planes, width_z)
    zs = shape(comps, ROWS, cross)
    start, uz, xlo, xhi, *msgs = call(
        functools.partial(assemble_kernel, planes, width_y, width_z),
        (full, fullz, xs, xs, ys, ys, zs, zs),
        [pltpu.VMEM(((2 + planes + reach) * ROWS, width_z), jnp.float32)],
        5,
    )(place, flat, ahead, behind, fresh)

    def plain(*dims):
        return pltpu.VMEM(dims, jnp.float32)

    rows_x = (planes + 2 * HALO) * ROWS
    rows_y = (width_y + 2 * HALO) * planes
    rows_z = width_z + 2 * ROWS
    zvecs = width_z // ROWS
    scratch = (
        [plain(comps, 2 * HALO * ROWS, width_z)]
        + [plain(rows_x, width_z)] * 3 + [plain((planes + 1) * ROWS, width_z)]
        + [plain(rows_y, width_z)] * 3 + [plain((width_y + 1) * planes, width_z)]
        + [plain(rows_z, cross)] * 3 + [plain((zvecs + 1) * ROWS, cross)]
        + [plain(3, cross, width_z), plain(comps, cross, width_z), plain(comps, cross, width_z),
           plain(comps, width_z, cross)]
    )
    current = start
    for stage in (1, 2, 3):
        ylo = moved(msgs[0], "gy", 1, True)
        yhi = moved(msgs[1], "gy", -1, True)
        zlo = moved(msgs[2], "gz", 1, True)
        zhi = moved(msgs[3], "gz", -1, True)
        outs = (full,)
        if stage < 3:
            outs = (full, fullz) + (xs,) * x_msgs + (ys, ys, zs, zs)
        current, *rest = call(
            functools.partial(stage_kernel, stage, planes, width_y, width_z, x_msgs),
            outs, scratch, 11,
        )(place, current, uz, start, fresh, xlo, xhi, ylo, yhi, zlo, zhi)
        if stage < 3:
            uz, *rest = rest
            msgs = rest[x_msgs:]
            if swap:
                xlo = xhi = lax.ppermute(rest[0], "tube", [(0, 1), (1, 0)])
            else:
                xhi = moved(rest[0], "tube", -1, False)
                xlo = moved(rest[1], "tube", 1, False)

    vmem = pl.BlockSpec(memory_space=pltpu.VMEM)
    reacted = pl.pallas_call(
        functools.partial(chemistry_kernel, planes, 4),
        out_shape=full,
        in_specs=[vmem, vmem],
        out_specs=vmem,
        compiler_params=pltpu.CompilerParams(vmem_limit_bytes=48 * 1024 * 1024),
    )(current, substeps.reshape(cross, width_z))
    return reacted.reshape(state.shape)


def solution(mesh):
    return jax.shard_map(
        on_device,
        mesh=mesh,
        in_specs=(P(None, "tube", "gy", "gz"), P(None, "gy", "gz"), P("tube", "gy", "gz"), P()),
        out_specs=P(None, "tube", "gy", "gz"),
        check_vma=False,
    )
```

profile of v0, /device:TPU:0, one launch (start us, length us, event | category | flops | bytes accessed | tf_op | source)
XLA Modules:
  0.0 97.5 jit_solution(3699886327495797689)
XLA Ops:
  0.0 1.5 %slice_select_fusion = f32[13,120,128]{2,1,0:T(8,128)S(1)} fusion(f32[13,128,128]{2,1,0:T(8,128)} %bitcast.7, pred[]{:T(512)S(6)} %eq.4), kind=kLoop, calls=%fused_computation | loop fusion | flops 199680 | bytes 2396161 | tf_op jit(solution)/shard_map/jit(_where)/select_n | solution.py:504
  1.5 3.0 %collective-permute-start = (f32[13,120,128]{2,1,0:T(8,128)S(1)}, f32[13,120,128]{2,1,0:T(8,128)S(1)}, u32[]{:S(2)}, u32[]{:S(2)}) collective-permute-start(f32[13,120,128]{2,1,0:T(8,128)S(1)} %slice_select_fusion), channel_id=1, source_target_pairs={{0,16},{16,0},{1,17},{17,1},{2,18},{18,2},{3,19},{19,3},{4,20},{20... | collective-permute-start | bytes 2396168 | tf_op jit(solution)/shard_map/ppermute | solution.py:505
  5.2 0.1 stack.15.place
  5.3 17.1 %collective-permute-done.ahead_ref = f32[13,120,128]{2,1,0:T(8,128)S(1)} collective-permute-done((f32[13,120,128]{2,1,0:T(8,128)S(1)}, f32[13,120,128]{2,1,0:T(8,128)S(1)}, u32[]{:S(2)}, u32[]{:S(2)}) %collective-permute-start) | collective-permute-done | bytes 798752 | tf_op jit(solution)/shard_map/ppermute | solution.py:505
  22.4 2.1 %shard_map.46 = (f32[13,128,128]{2,1,0:T(8,128)S(1)}, f32[13,144,128]{2,1,0:T(8,128)S(1)}, f32[13,24,128]{2,1,0:T(8,128)S(1)}, f32[13,24,128]{2,1,0:T(8,128)S(1)...) custom-call(s32[5]{0:T(128)S(1)} %stack.15.place, ...), custom_call_target="tpu_custom_call" | custom-call | tf_op jit(solution)/shard_map/pallas_call | solution.py:516
  24.5 0.1 collective-permute-start.1
  24.6 1.7 %collective-permute-start.2 = (f32[13,48,128]{2,1,0:T(8,128)S(1)}, f32[13,48,128]{2,1,0:T(8,128)S(1)}, u32[]{:S(2)}, u32[]{:S(2)}) collective-permute-start(f32[13,48,128]{2,1,0:T(8,128)S(1)} %get-tuple-element.32), channel_id=1, source_target_pairs={{0,12},{4,0},{8,4},{12,8},{1,13},{5,1},{9,5},{13,9},{2,14},{6,2},{... | collective-permute-start | bytes 958472 | tf_op jit(solution)/shard_map/ppermute | solution.py:486
  26.3 1.8 %collective-permute-start.3 = (f32[13,8,128]{2,1,0:T(8,128)S(1)}, f32[13,8,128]{2,1,0:T(8,128)S(1)}, u32[]{:S(2)}, u32[]{:S(2)}) collective-permute-start(f32[13,8,128]{2,1,0:T(8,128)S(1)} %get-tuple-element.33), channel_id=1, source_target_pairs={{0,1},{1,2},{2,3},{3,0},{4,5},{5,6},{6,7},{7,4},{8,9},{9,10},{10,1... | collective-permute-start | bytes 159752 | tf_op jit(solution)/shard_map/ppermute | solution.py:486
  28.2 2.0 %collective-permute-start.4 = (f32[13,8,128]{2,1,0:T(8,128)S(1)}, f32[13,8,128]{2,1,0:T(8,128)S(1)}, u32[]{:S(2)}, u32[]{:S(2)}) collective-permute-start(f32[13,8,128]{2,1,0:T(8,128)S(1)} %get-tuple-element.34), channel_id=1, source_target_pairs={{0,3},{1,0},{2,1},{3,2},{4,7},{5,4},{6,5},{7,6},{8,11},{9,8},{10,9... | collective-permute-start | bytes 159752 | tf_op jit(solution)/shard_map/ppermute | solution.py:486
  30.2 2.2 %collective-permute-done.3.zlo_ref = f32[13,8,128]{2,1,0:T(8,128)S(1)} collective-permute-done((f32[13,8,128]{2,1,0:T(8,128)S(1)}, f32[13,8,128]{2,1,0:T(8,128)S(1)}, u32[]{:S(2)}, u32[]{:S(2)}) %collective-permute-start.3) | collective-permute-done | bytes 53280 | tf_op jit(solution)/shard_map/ppermute | solution.py:486
  32.4 0.5 collective-permute-done.4.zhi_ref
  32.9 0.0 collective-permute-done.1.ylo_ref
  32.9 0.9 collective-permute-done.2.yhi_ref
  33.7 13.7 %shard_map.47 = (f32[13,128,128]{2,1,0:T(8,128)S(1)}, f32[13,144,128]{2,1,0:T(8,128)S(1)}, f32[13,24,128]{2,1,0:T(8,128)S(1)}, f32[13,48,128]{2,1,0:T(8,128)S(1)...) custom-call(s32[5]{0:T(128)S(1)} %stack.15.place, ...), custom_call_target="tpu_custom_call" | custom-call | tf_op jit(solution)/shard_map/pallas_call | solution.py:547
  47.5 0.9 copy-done.1
  48.4 0.5 collective-permute-start.6
  49.0 1.4 %collective-permute-start.7 = (f32[13,48,128]{2,1,0:T(8,128)S(1)}, f32[13,48,128]{2,1,0:T(8,128)S(1)}, u32[]{:S(2)}, u32[]{:S(2)}) collective-permute-start(f32[13,48,128]{2,1,0:T(8,128)S(1)} %get-tuple-element.39), channel_id=1, source_target_pairs={{0,12},{4,0},{8,4},{12,8},{1,13},{5,1},{9,5},{13,9},{2,14},{6,2},{... | collective-permute-start | bytes 958472 | tf_op jit(solution)/shard_map/ppermute | solution.py:486
  50.3 1.5 %collective-permute-start.5 = (f32[13,24,128]{2,1,0:T(8,128)S(1)}, f32[13,24,128]{2,1,0:T(8,128)S(1)}, u32[]{:S(2)}, u32[]{:S(2)}) collective-permute-start(f32[13,24,128]{2,1,0:T(8,128)S(1)} %get-tuple-element.37), channel_id=1, source_target_pairs={{0,16},{16,0},{1,17},{17,1},{2,18},{18,2},{3,19},{19,3},{4,20},{20... | collective-permute-start | bytes 479240 | tf_op jit(solution)/shard_map/ppermute | solution.py:555
  51.8 1.6 %collective-permute-start.8 = (f32[13,8,128]{2,1,0:T(8,128)S(1)}, f32[13,8,128]{2,1,0:T(8,128)S(1)}, u32[]{:S(2)}, u32[]{:S(2)}) collective-permute-start(f32[13,8,128]{2,1,0:T(8,128)S(1)} %get-tuple-element.40), channel_id=1, source_target_pairs={{0,1},{1,2},{2,3},{3,0},{4,5},{5,6},{6,7},{7,4},{8,9},{9,10},{10,1... | collective-permute-start | bytes 159752 | tf_op jit(solution)/shard_map/ppermute | solution.py:486
  53.4 2.2 %collective-permute-start.9 = (f32[13,8,128]{2,1,0:T(8,128)S(1)}, f32[13,8,128]{2,1,0:T(8,128)S(1)}, u32[]{:S(2)}, u32[]{:S(2)}) collective-permute-start(f32[13,8,128]{2,1,0:T(8,128)S(1)} %get-tuple-element.41), channel_id=1, source_target_pairs={{0,3},{1,0},{2,1},{3,2},{4,7},{5,4},{6,5},{7,6},{8,11},{9,8},{10,9... | collective-permute-start | bytes 159752 | tf_op jit(solution)/shard_map/ppermute | solution.py:486
  55.6 2.5 %collective-permute-done.8.zlo_ref = f32[13,8,128]{2,1,0:T(8,128)S(1)} collective-permute-done((f32[13,8,128]{2,1,0:T(8,128)S(1)}, f32[13,8,128]{2,1,0:T(8,128)S(1)}, u32[]{:S(2)}, u32[]{:S(2)}) %collective-permute-start.8) | collective-permute-done | bytes 53280 | tf_op jit(solution)/shard_map/ppermute | solution.py:486
  58.1 0.0 collective-permute-done.5.xlo_ref.xhi_ref
  58.2 14.5 %shard_map.48 = (f32[13,128,128]{2,1,0:T(8,128)S(1)}, f32[13,144,128]{2,1,0:T(8,128)S(1)}, f32[13,24,128]{2,1,0:T(8,128)S(1)}, f32[13,48,128]{2,1,0:T(8,128)S(1)...) custom-call(s32[5]{0:T(128)S(1)} %stack.15.place, ...), custom_call_target="tpu_custom_call" | custom-call | tf_op jit(solution)/shard_map/pallas_call | solution.py:547
  72.6 0.1 collective-permute-start.11
  72.8 1.7 %collective-permute-start.12 = (f32[13,48,128]{2,1,0:T(8,128)S(1)}, f32[13,48,128]{2,1,0:T(8,128)S(1)}, u32[]{:S(2)}, u32[]{:S(2)}) collective-permute-start(f32[13,48,128]{2,1,0:T(8,128)S(1)} %get-tuple-element.46), channel_id=1, source_target_pairs={{0,12},{4,0},{8,4},{12,8},{1,13},{5,1},{9,5},{13,9},{2,14},{6,2},{... | collective-permute-start | bytes 958472 | tf_op jit(solution)/shard_map/ppermute | solution.py:486
  74.5 1.0 %collective-permute-start.10 = (f32[13,24,128]{2,1,0:T(8,128)S(1)}, f32[13,24,128]{2,1,0:T(8,128)S(1)}, u32[]{:S(2)}, u32[]{:S(2)}) collective-permute-start(f32[13,24,128]{2,1,0:T(8,128)S(1)} %get-tuple-element.44), channel_id=1, source_target_pairs={{0,16},{16,0},{1,17},{17,1},{2,18},{18,2},{3,19},{19,3},{4,20},{20... | collective-permute-start | bytes 479240 | tf_op jit(solution)/shard_map/ppermute | solution.py:555
  75.5 1.6 %collective-permute-start.13 = (f32[13,8,128]{2,1,0:T(8,128)S(1)}, f32[13,8,128]{2,1,0:T(8,128)S(1)}, u32[]{:S(2)}, u32[]{:S(2)}) collective-permute-start(f32[13,8,128]{2,1,0:T(8,128)S(1)} %get-tuple-element.47), channel_id=1, source_target_pairs={{0,1},{1,2},{2,3},{3,0},{4,5},{5,6},{6,7},{7,4},{8,9},{9,10},{10,1... | collective-permute-start | bytes 159752 | tf_op jit(solution)/shard_map/ppermute | solution.py:486
  77.0 2.2 %collective-permute-start.14 = (f32[13,8,128]{2,1,0:T(8,128)S(1)}, f32[13,8,128]{2,1,0:T(8,128)S(1)}, u32[]{:S(2)}, u32[]{:S(2)}) collective-permute-start(f32[13,8,128]{2,1,0:T(8,128)S(1)} %get-tuple-element.48), channel_id=1, source_target_pairs={{0,3},{1,0},{2,1},{3,2},{4,7},{5,4},{6,5},{7,6},{8,11},{9,8},{10,9... | collective-permute-start | bytes 159752 | tf_op jit(solution)/shard_map/ppermute | solution.py:486
  79.3 2.5 %collective-permute-done.13.zlo_ref = f32[13,8,128]{2,1,0:T(8,128)S(1)} collective-permute-done((f32[13,8,128]{2,1,0:T(8,128)S(1)}, f32[13,8,128]{2,1,0:T(8,128)S(1)}, u32[]{:S(2)}, u32[]{:S(2)}) %collective-permute-start.13) | collective-permute-done | bytes 53280 | tf_op jit(solution)/shard_map/ppermute | solution.py:486
  81.8 0.0 copy-start.3
  81.8 12.9 %shard_map.49.third_ref = f32[13,128,128]{2,1,0:T(8,128)S(1)} custom-call(s32[5]{0:T(128)S(1)} %stack.15.place, f32[13,128,128]{2,1,0:T(8,128)S(1)} %get-tuple-element.42.u_ref, f32[13,144,128]{2,1,0:T(8,128)S(1)} %get-tuple-element.43.uz_ref, f32[13,128,128]{2,1,0:T(8,128)S(1)} %get-tuple-element.27.u_ref.start_ref, f32[13,8,128]{2,1,0:T(8,128)S(1)} %copy-done.2, ...), custom_call_target="tpu_custom_call" | custom-call | tf_op jit(solution)/shard_map/pallas_call | solution.py:547
  94.7 2.8 %shard_map.50 = f32[13,128,128]{2,1,0:T(8,128)} custom-call(f32[13,128,128]{2,1,0:T(8,128)S(1)} %shard_map.49.third_ref, s32[128,128]{1,0:T(8,128)S(1)} %bitcast.9), custom_call_target="tpu_custom_call" | custom-call | tf_op jit(solution)/shard_map/pallas_call | solution.py:561
  (14 shorter events, 0.0 us)
Async XLA Ops:
  0.0 22.4 %copy-start = (f32[13,16,8,128]{3,2,1,0:T(8,128)S(1)}, f32[13,16,8,128]{3,2,1,0:T(8,128)}, u32[]{:S(2)}) copy-start(f32[13,16,8,128]{3,2,1,0:T(8,128)} %param.4) | copy-start | bytes 2555908
  1.5 20.8 %collective-permute-start = (f32[13,120,128]{2,1,0:T(8,128)S(1)}, f32[13,120,128]{2,1,0:T(8,128)S(1)}, u32[]{:S(2)}, u32[]{:S(2)}) collective-permute-start(f32[13,120,128]{2,1,0:T(8,128)S(1)} %slice_select_fusion), channel_id=1, source_target_pairs={{0,16},{16,0},{1,17},{17,1},{2,18},{18,2},{3,19},{19,3},{4,20},{20... | collective-permute-start | bytes 2396168 | tf_op jit(solution)/shard_map/ppermute | solution.py:505
  5.3 17.1 %copy-start.2 = (f32[13,8,128]{2,1,0:T(8,128)S(1)}, f32[13,8,128]{2,1,0:T(8,128)}, u32[]{:S(2)}) copy-start(f32[13,8,128]{2,1,0:T(8,128)} %fresh_ref.7) | copy-start | bytes 159748
  24.5 8.3 %collective-permute-start.1 = (f32[13,48,128]{2,1,0:T(8,128)S(1)}, f32[13,48,128]{2,1,0:T(8,128)S(1)}, u32[]{:S(2)}, u32[]{:S(2)}) collective-permute-start(f32[13,48,128]{2,1,0:T(8,128)S(1)} %get-tuple-element.31), channel_id=1, source_target_pairs={{0,4},{4,8},{8,12},{12,0},{1,5},{5,9},{9,13},{13,1},{2,6},{6,10},{... | collective-permute-start | bytes 958472 | tf_op jit(solution)/shard_map/ppermute | solution.py:486
  24.6 9.1 %collective-permute-start.2 = (f32[13,48,128]{2,1,0:T(8,128)S(1)}, f32[13,48,128]{2,1,0:T(8,128)S(1)}, u32[]{:S(2)}, u32[]{:S(2)}) collective-permute-start(f32[13,48,128]{2,1,0:T(8,128)S(1)} %get-tuple-element.32), channel_id=1, source_target_pairs={{0,12},{4,0},{8,4},{12,8},{1,13},{5,1},{9,5},{13,9},{2,14},{6,2},{... | collective-permute-start | bytes 958472 | tf_op jit(solution)/shard_map/ppermute | solution.py:486
  26.3 6.0 %collective-permute-start.3 = (f32[13,8,128]{2,1,0:T(8,128)S(1)}, f32[13,8,128]{2,1,0:T(8,128)S(1)}, u32[]{:S(2)}, u32[]{:S(2)}) collective-permute-start(f32[13,8,128]{2,1,0:T(8,128)S(1)} %get-tuple-element.33), channel_id=1, source_target_pairs={{0,1},{1,2},{2,3},{3,0},{4,5},{5,6},{6,7},{7,4},{8,9},{9,10},{10,1... | collective-permute-start | bytes 159752 | tf_op jit(solution)/shard_map/ppermute | solution.py:486
  28.2 4.7 %collective-permute-start.4 = (f32[13,8,128]{2,1,0:T(8,128)S(1)}, f32[13,8,128]{2,1,0:T(8,128)S(1)}, u32[]{:S(2)}, u32[]{:S(2)}) collective-permute-start(f32[13,8,128]{2,1,0:T(8,128)S(1)} %get-tuple-element.34), channel_id=1, source_target_pairs={{0,3},{1,0},{2,1},{3,2},{4,7},{5,4},{6,5},{7,6},{8,11},{9,8},{10,9... | collective-permute-start | bytes 159752 | tf_op jit(solution)/shard_map/ppermute | solution.py:486
  47.5 1.0 copy-start.1
  48.4 9.7 %collective-permute-start.6 = (f32[13,48,128]{2,1,0:T(8,128)S(1)}, f32[13,48,128]{2,1,0:T(8,128)S(1)}, u32[]{:S(2)}, u32[]{:S(2)}) collective-permute-start(f32[13,48,128]{2,1,0:T(8,128)S(1)} %get-tuple-element.38), channel_id=1, source_target_pairs={{0,4},{4,8},{8,12},{12,0},{1,5},{5,9},{9,13},{13,1},{2,6},{6,10},{... | collective-permute-start | bytes 958472 | tf_op jit(solution)/shard_map/ppermute | solution.py:486
  49.0 9.2 %collective-permute-start.7 = (f32[13,48,128]{2,1,0:T(8,128)S(1)}, f32[13,48,128]{2,1,0:T(8,128)S(1)}, u32[]{:S(2)}, u32[]{:S(2)}) collective-permute-start(f32[13,48,128]{2,1,0:T(8,128)S(1)} %get-tuple-element.39), channel_id=1, source_target_pairs={{0,12},{4,0},{8,4},{12,8},{1,13},{5,1},{9,5},{13,9},{2,14},{6,2},{... | collective-permute-start | bytes 958472 | tf_op jit(solution)/shard_map/ppermute | solution.py:486
  50.3 7.8 %collective-permute-start.5 = (f32[13,24,128]{2,1,0:T(8,128)S(1)}, f32[13,24,128]{2,1,0:T(8,128)S(1)}, u32[]{:S(2)}, u32[]{:S(2)}) collective-permute-start(f32[13,24,128]{2,1,0:T(8,128)S(1)} %get-tuple-element.37), channel_id=1, source_target_pairs={{0,16},{16,0},{1,17},{17,1},{2,18},{18,2},{3,19},{19,3},{4,20},{20... | collective-permute-start | bytes 479240 | tf_op jit(solution)/shard_map/ppermute | solution.py:555
  51.8 6.3 %collective-permute-start.8 = (f32[13,8,128]{2,1,0:T(8,128)S(1)}, f32[13,8,128]{2,1,0:T(8,128)S(1)}, u32[]{:S(2)}, u32[]{:S(2)}) collective-permute-start(f32[13,8,128]{2,1,0:T(8,128)S(1)} %get-tuple-element.40), channel_id=1, source_target_pairs={{0,1},{1,2},{2,3},{3,0},{4,5},{5,6},{6,7},{7,4},{8,9},{9,10},{10,1... | collective-permute-start | bytes 159752 | tf_op jit(solution)/shard_map/ppermute | solution.py:486
  53.4 4.7 %collective-permute-start.9 = (f32[13,8,128]{2,1,0:T(8,128)S(1)}, f32[13,8,128]{2,1,0:T(8,128)S(1)}, u32[]{:S(2)}, u32[]{:S(2)}) collective-permute-start(f32[13,8,128]{2,1,0:T(8,128)S(1)} %get-tuple-element.41), channel_id=1, source_target_pairs={{0,3},{1,0},{2,1},{3,2},{4,7},{5,4},{6,5},{7,6},{8,11},{9,8},{10,9... | collective-permute-start | bytes 159752 | tf_op jit(solution)/shard_map/ppermute | solution.py:486
  72.6 9.2 %collective-permute-start.11 = (f32[13,48,128]{2,1,0:T(8,128)S(1)}, f32[13,48,128]{2,1,0:T(8,128)S(1)}, u32[]{:S(2)}, u32[]{:S(2)}) collective-permute-start(f32[13,48,128]{2,1,0:T(8,128)S(1)} %get-tuple-element.45), channel_id=1, source_target_pairs={{0,4},{4,8},{8,12},{12,0},{1,5},{5,9},{9,13},{13,1},{2,6},{6,10},{... | collective-permute-start | bytes 958472 | tf_op jit(solution)/shard_map/ppermute | solution.py:486
  72.8 9.0 %collective-permute-start.12 = (f32[13,48,128]{2,1,0:T(8,128)S(1)}, f32[13,48,128]{2,1,0:T(8,128)S(1)}, u32[]{:S(2)}, u32[]{:S(2)}) collective-permute-start(f32[13,48,128]{2,1,0:T(8,128)S(1)} %get-tuple-element.46), channel_id=1, source_target_pairs={{0,12},{4,0},{8,4},{12,8},{1,13},{5,1},{9,5},{13,9},{2,14},{6,2},{... | collective-permute-start | bytes 958472 | tf_op jit(solution)/shard_map/ppermute | solution.py:486
  74.5 7.4 %collective-permute-start.10 = (f32[13,24,128]{2,1,0:T(8,128)S(1)}, f32[13,24,128]{2,1,0:T(8,128)S(1)}, u32[]{:S(2)}, u32[]{:S(2)}) collective-permute-start(f32[13,24,128]{2,1,0:T(8,128)S(1)} %get-tuple-element.44), channel_id=1, source_target_pairs={{0,16},{16,0},{1,17},{17,1},{2,18},{18,2},{3,19},{19,3},{4,20},{20... | collective-permute-start | bytes 479240 | tf_op jit(solution)/shard_map/ppermute | solution.py:555
  75.5 6.3 %collective-permute-start.13 = (f32[13,8,128]{2,1,0:T(8,128)S(1)}, f32[13,8,128]{2,1,0:T(8,128)S(1)}, u32[]{:S(2)}, u32[]{:S(2)}) collective-permute-start(f32[13,8,128]{2,1,0:T(8,128)S(1)} %get-tuple-element.47), channel_id=1, source_target_pairs={{0,1},{1,2},{2,3},{3,0},{4,5},{5,6},{6,7},{7,4},{8,9},{9,10},{10,1... | collective-permute-start | bytes 159752 | tf_op jit(solution)/shard_map/ppermute | solution.py:486
  77.0 4.8 %collective-permute-start.14 = (f32[13,8,128]{2,1,0:T(8,128)S(1)}, f32[13,8,128]{2,1,0:T(8,128)S(1)}, u32[]{:S(2)}, u32[]{:S(2)}) collective-permute-start(f32[13,8,128]{2,1,0:T(8,128)S(1)} %get-tuple-element.48), channel_id=1, source_target_pairs={{0,3},{1,0},{2,1},{3,2},{4,7},{5,4},{6,5},{7,6},{8,11},{9,8},{10,9... | collective-permute-start | bytes 159752 | tf_op jit(solution)/shard_map/ppermute | solution.py:486
  81.8 12.9 %copy-start.3 = (s32[16,8,128]{2,1,0:T(8,128)S(1)}, s32[16,8,128]{2,1,0:T(8,128)}, u32[]{:S(2)}) copy-start(s32[16,8,128]{2,1,0:T(8,128)} %param.6) | copy-start | bytes 196612
where the time goes:
time: 97.7 us; the launch traced here: 97.5 us
  Pallas kernels  46 us (47%)
  waiting for transfers between devices  25.6 us (26%)
  starting transfers between devices  22.5 us (23%)
  other arithmetic  1.54 us (2%)
  local copies, waits for them, and re-layouts  1.05 us (1%)
    pallas_call x3, Pallas kernels, on_device(): call(functools.partial(stage_kernel, stage, planes, width_y, width_z, x_m...  41.1 us
    ppermute x1, waiting for transfers between devices, on_device(): ahead = lax.ppermute(out, 'tube', [(0, 1), (1, 0)])  17.1 us
    ppermute x12, starting transfers between devices, moved(): return lax.ppermute(value, axis, pairs)  17 us
    ppermute x12, waiting for transfers between devices, moved(): return lax.ppermute(value, axis, pairs)  8.55 us
    ppermute x1, starting transfers between devices, on_device(): ahead = lax.ppermute(out, 'tube', [(0, 1), (1, 0)])  3 us
    pallas_call x1, Pallas kernels, on_device(): pl.pallas_call(functools.partial(chemistry_kernel, planes, 4), out_shape=...  2.76 us
    ppermute x2, starting transfers between devices, on_device(): xlo = xhi = lax.ppermute(rest[0], 'tube', [(0, 1), (1, 0)])  2.49 us
    pallas_call x1, Pallas kernels, on_device(): call(functools.partial(assemble_kernel, planes, width_y, width_z), (full,...  2.15 us
  transfers between devices with their start and end apart: 15, of which 6 were waited for; matrix products, arithmetic and copies ran while one was open for 0% of the time, Pallas kernels for 0%

commit v1 on v0

--- a/solution.py
+++ b/solution.py
@@ -126,25 +126,106 @@
     return (u + pressure()) * speed
 
 
-def alphas(speed, faces, alpha_ref, rows):
-    values = memo(lambda i: speed[pl.ds(i * rows, ROWS), :])
-    for j in range(faces):
+def own_thermo(planes, width_y, u_ref, x_refs, y_refs, z_refs, tmp):
+    def own(i, _):
+        for k in range(2):
+            p = i * 2 + k
+            here = pl.ds(pl.multiple_of(p * ROWS, ROWS), ROWS)
+            u = [u_ref[c, here, :] for c in range(NCOMP)]
+            back, pressure, sound = thermo(u)
+            back, sound = SCALE * back, SCALE * sound
+            across = pl.ds(p, width_y, stride=planes)
+            for d, where in ((0, here), (1, across), (2, here)):
+                speed = u[9 + d] * back
+                for n, value in enumerate((speed, pressure, jnp.abs(speed) + sound)):
+                    if d == 2:
+                        tmp[n, where, :] = value
+                    else:
+                        (x_refs, y_refs)[d][n][where, :] = value
+        return 0
+
+    lax.fori_loop(0, planes // 2, own, 0)
+    for n in range(3):
+        z_refs[n][pl.ds(ROWS, tmp.shape[2]), :] = tmp[n].T
+
+
+def inner_kernel(
+    planes, width_y, width_z, u_ref, uz_ref,
+    ux, px, ax, uy, py, ay, uz, pz, az, accx, accy, accz, alx, aly, alz, tmp,
+):
+    groups = planes // ROWS
+    zvecs = width_z // ROWS
+    own_thermo(planes, width_y, u_ref, (ux, px, ax), (uy, py, ay), (uz, pz, az), tmp)
+
+    def xvec(ref):
+        return lambda i: ref[pl.ds((i - HALO) * ROWS, ROWS), :]
+
+    def yvec(ref, g):
+        return lambda i: ref[pl.ds((i - HALO) * planes + g * ROWS, ROWS), :]
+
+    def zvec(ref):
+        return lambda i: ref[pl.ds(ROWS - HALO + i, ROWS, stride=zvecs), :]
+
+    largest(xvec(ax), range(HALO, planes - HALO + 1), alx, lambda j: j * ROWS)
+    for g in range(groups):
+        largest(yvec(ay, g), range(HALO, width_y - HALO + 1), aly,
+                lambda j: j * planes + g * ROWS)
+    largest(zvec(az), range(HALO, zvecs - HALO + 1), alz, lambda j: j * ROWS)
+
+    def inner(n, cells, speed, pressure, kind, alpha, put):
+        cells = memo(cells)
+        fluxes = memo(lambda i: flux_of(cells(i), speed(i), lambda: pressure(i), kind))
+        out = sweep(cells, fluxes, alpha, HALO, n - HALO)
+        put(HALO - 1, out[HALO])
+        for i in range(HALO, n - HALO):
+            put(i, out[i + 1] - out[i])
+        put(n - HALO, out[n - HALO])
+
+    def x_body(c, kind):
+        def put(i, value):
+            accx[c, pl.ds(i * ROWS, ROWS), :] = value
+        inner(planes, lambda i: u_ref[c, pl.ds((i - HALO) * ROWS, ROWS), :], xvec(ux), xvec(px),
+              kind, lambda j: alx[pl.ds(j * ROWS, ROWS), :], put)
+
+    for_components(1, x_body)
+
+    def z_body(c, kind):
+        def put(i, value):
+            accz[c, pl.ds(i, ROWS, stride=zvecs), :] = value
+        inner(zvecs, lambda i: uz_ref[c, pl.ds(ROWS - HALO + i, ROWS, stride=zvecs), :],
+              zvec(uz), zvec(pz), kind, lambda j: alz[pl.ds(j * ROWS, ROWS), :], put)
+
+    for_components(3, z_body)
+
+    def y_body(c, kind):
+        for g in range(groups):
+            def put(i, value, g=g):
+                accy[c, pl.ds(g * ROWS * width_y + i, ROWS, stride=width_y), :] = value
+            def cell(i, g=g):
+                return u_ref[c, pl.ds(g * ROWS * width_y + i - HALO, ROWS, stride=width_y), :]
+            inner(width_y, cell, yvec(uy, g), yvec(py, g), kind,
+                  lambda j: aly[pl.ds(j * planes + g * ROWS, ROWS), :], put)
+
+    for_components(2, y_body)
+
+
+def largest(speed, faces, ref, place):
+    values = memo(speed)
+    for j in faces:
         top = values(j)
         for k in range(1, 6):
             top = jnp.maximum(top, values(j + k))
-        alpha_ref[pl.ds(j * rows, ROWS), :] = top
-
-
-def stage_kernel(
+        ref[pl.ds(place(j), ROWS), :] = top
+
+
+def outer_kernel(
     stage, planes, width_y, width_z, x_msgs, place,
     u_ref, uz_ref, start_ref, fresh_ref, xlo_ref, xhi_ref, ylo_ref, yhi_ref, zlo_ref, zhi_ref,
-    *refs,
+    ux, px, ax, uy, py, ay, uz, pz, az, accx, accy, accz, *refs,
 ):
     groups = planes // ROWS
     zvecs = width_z // ROWS
-    tubes = place[1]
-    tube = place[0]
-    first = stage == 1
+    tube, tubes = place[0], place[1]
     last = stage == 3
     refs = list(refs)
     new_ref = refs.pop(0)
@@ -152,144 +233,145 @@
         newz_ref = refs.pop(0)
         xmsg_refs = [refs.pop(0) for _ in range(x_msgs)]
         ymsg_lo, ymsg_hi, zmsg_lo, zmsg_hi = [refs.pop(0) for _ in range(4)]
-    (
-        xh, ux, px, ax, alx, uy, py, ay, aly, uz, pz, az, alz, tmp, accx, accy, accz,
-    ) = refs
+    xh, gx, gy, gz, alx, aly, alz, edgex, edgey, edgez = refs
 
     def ghosts(c, _):
         for k in range(HALO):
             here = pl.ds(k * ROWS, ROWS)
-            lo, hi = xlo_ref[c, here, :], xhi_ref[c, here, :]
-            if not first:
-                lo = jnp.where(tube == 0, u_ref[c, pl.ds(0, ROWS), :], lo)
-                hi = jnp.where(tube == tubes - 1, fresh_ref[c], hi)
+            lo = jnp.where(tube == 0, u_ref[c, pl.ds(0, ROWS), :], xlo_ref[c, here, :])
+            hi = jnp.where(tube == tubes - 1, fresh_ref[c], xhi_ref[c, here, :])
             xh[c, here, :] = lo
             xh[c, pl.ds((HALO + k) * ROWS, ROWS), :] = hi
         return 0
 
     lax.fori_loop(0, NCOMP, ghosts, 0)
 
-    def own(i, _):
-        for k in range(2):
-            p = i * 2 + k
-            here = pl.ds(pl.multiple_of(p * ROWS, ROWS), ROWS)
-            u = [u_ref[c, here, :] for c in range(NCOMP)]
-            back, pressure, sound = thermo(u)
-            back, sound = SCALE * back, SCALE * sound
-            there = pl.ds(pl.multiple_of((p + HALO) * ROWS, ROWS), ROWS)
-            speeds = [u[9 + d] * back for d in range(3)]
-            ux[there, :] = speeds[0]
-            px[there, :] = pressure
-            ax[there, :] = jnp.abs(speeds[0]) + sound
-            ystart = pl.ds(HALO * planes + p, width_y, stride=planes)
-            uy[ystart, :] = speeds[1]
-            py[ystart, :] = pressure
-            ay[ystart, :] = jnp.abs(speeds[1]) + sound
-            tmp[0, here, :] = speeds[2]
-            tmp[1, here, :] = pressure
-            tmp[2, here, :] = jnp.abs(speeds[2]) + sound
-        return 0
-
-    lax.fori_loop(0, planes // 2, own, 0)
-    for ref, k in ((uz, 0), (pz, 1), (az, 2)):
-        ref[pl.ds(ROWS, width_z), :] = tmp[k].T
-
-    def ghost_thermo(u, d, speed_ref, pressure_ref, top_ref, row):
+    def ghost_thermo(u, d, ref, row):
         back, pressure, sound = thermo(u)
         speed = u[9 + d] * (SCALE * back)
-        speed_ref[pl.ds(row, ROWS), :] = speed
-        pressure_ref[pl.ds(row, ROWS), :] = pressure
-        top_ref[pl.ds(row, ROWS), :] = jnp.abs(speed) + SCALE * sound
+        for n, value in enumerate((speed, pressure, jnp.abs(speed) + SCALE * sound)):
+            ref[n, pl.ds(row, ROWS), :] = value
 
     for k in range(2 * HALO):
-        row = k if k < HALO else planes + k
-        u = [xh[c, pl.ds(k * ROWS, ROWS), :] for c in range(NCOMP)]
-        ghost_thermo(u, 0, ux, px, ax, row * ROWS)
-    for ref, offset in ((ylo_ref, 0), (yhi_ref, HALO + width_y)):
+        ghost_thermo([xh[c, pl.ds(k * ROWS, ROWS), :] for c in range(NCOMP)], 0, gx, k * ROWS)
+    for ref, offset in ((ylo_ref, 0), (yhi_ref, HALO)):
         def ghost_y(k, _, ref=ref, offset=offset):
             for g in range(groups):
-                u = [ref[c, pl.ds(k * planes + g * ROWS, ROWS), :] for c in range(NCOMP)]
-                ghost_thermo(u, 1, uy, py, ay, (offset + k) * planes + g * ROWS)
+                row = pl.multiple_of(k * planes + g * ROWS, ROWS)
+                u = [ref[c, pl.ds(row, ROWS), :] for c in range(NCOMP)]
+                ghost_thermo(u, 1, gy, pl.multiple_of(offset * planes + row, ROWS))
             return 0
         lax.fori_loop(0, HALO, ghost_y, 0)
-    for ref, row in ((zlo_ref, 0), (zhi_ref, ROWS + width_z)):
-        u = [ref[c] for c in range(NCOMP)]
-        ghost_thermo(u, 2, uz, pz, az, row)
-
-    alphas(ax, planes + 1, alx, ROWS)
+    ghost_thermo([zlo_ref[c] for c in range(NCOMP)], 2, gz, 0)
+    ghost_thermo([zhi_ref[c] for c in range(NCOMP)], 2, gz, ROWS)
+
+    def xvec(ref, n):
+        def load(i):
+            if HALO <= i < planes + HALO:
+                return ref[pl.ds((i - HALO) * ROWS, ROWS), :]
+            return gx[n, pl.ds((i if i < HALO else i - planes) * ROWS, ROWS), :]
+        return load
+
+    def yvec(ref, n, g):
+        def load(i):
+            if HALO <= i < width_y + HALO:
+                return ref[pl.ds((i - HALO) * planes + g * ROWS, ROWS), :]
+            return gy[n, pl.ds((i if i < HALO else i - width_y) * planes + g * ROWS, ROWS), :]
+        return load
+
+    row = lax.broadcasted_iota(jnp.int32, (ROWS, planes * width_y), 0)
+
+    def joined(i, load, lo, hi):
+        value = load(pl.ds(ROWS - HALO + i, ROWS, stride=zvecs))
+        if i < HALO:
+            return jnp.where(row == 0, lo(pl.ds(ROWS - HALO + i, 1)), value)
+        if i >= zvecs + HALO:
+            return jnp.where(row == ROWS - 1, hi(pl.ds(i - zvecs - HALO, 1)), value)
+        return value
+
+    def zvec(ref, n):
+        def load(i):
+            return joined(i, lambda s: ref[s, :], lambda s: gz[n, s, :],
+                          lambda s: gz[n, pl.ds(ROWS + s.start, 1), :])
+        return load
+
+    def ends(n):
+        return list(range(HALO)) + list(range(n - HALO + 1, n + 1))
+
+    largest(xvec(ax, 2), ends(planes), alx, lambda j: j * ROWS)
     for g in range(groups):
-        values = memo(lambda i: ay[pl.ds(i * planes + g * ROWS, ROWS), :])
-        for j in range(width_y + 1):
-            top = values(j)
-            for k in range(1, 6):
-                top = jnp.maximum(top, values(j + k))
-            aly[pl.ds(j * planes + g * ROWS, ROWS), :] = top
-
-    def zvec(ref, i):
-        return ref[pl.ds(ROWS - HALO + i, ROWS, stride=zvecs), :]
-
-    values_z = memo(lambda i: zvec(az, i))
-    for j in range(zvecs + 1):
-        top = values_z(j)
-        for k in range(1, 6):
-            top = jnp.maximum(top, values_z(j + k))
-        alz[pl.ds(j * ROWS, ROWS), :] = top
+        largest(yvec(ay, 2, g), ends(width_y), aly, lambda j: j * planes + g * ROWS)
+    largest(zvec(az, 2), ends(zvecs), alz, lambda j: j * ROWS)
+
+    def outer(n, cells, speed, pressure, kind, alpha, given, put):
+        cells = memo(cells)
+        fluxes = memo(lambda i: flux_of(cells(i), speed(i), lambda: pressure(i), kind))
+        out = sweep(cells, fluxes, alpha, 0, HALO - 1)
+        out[HALO] = given(HALO - 1)
+        for i in range(HALO):
+            put(i, out[i + 1] - out[i])
+        out = sweep(cells, fluxes, alpha, n - HALO + 1, n)
+        out[n - HALO] = given(n - HALO)
+        for i in range(n - HALO, n):
+            put(i, out[i + 1] - out[i])
 
     def x_body(c, kind):
         def cell(i):
             if HALO <= i < planes + HALO:
                 return u_ref[c, pl.ds((i - HALO) * ROWS, ROWS), :]
-            k = i if i < HALO else i - planes
-            return xh[c, pl.ds(k * ROWS, ROWS), :]
-        cells = memo(cell)
-        fluxes = memo(lambda i: flux_of(
-            cells(i), ux[pl.ds(i * ROWS, ROWS), :], lambda: px[pl.ds(i * ROWS, ROWS), :], kind))
-        out = sweep(cells, fluxes, lambda j: alx[pl.ds(j * ROWS, ROWS), :], 0, planes)
-        for i in range(planes):
-            accx[c, pl.ds(i * ROWS, ROWS), :] = out[i + 1] - out[i]
+            return xh[c, pl.ds((i if i < HALO else i - planes) * ROWS, ROWS), :]
+        def put(i, value):
+            edgex[c, pl.ds((i if i < HALO else i - planes + 2 * HALO) * ROWS, ROWS), :] = value
+        outer(planes, cell, xvec(ux, 0), xvec(px, 1), kind,
+              lambda j: alx[pl.ds(j * ROWS, ROWS), :],
+              lambda i: accx[c, pl.ds(i * ROWS, ROWS), :], put)
 
     for_components(1, x_body)
+
+    def z_body(c, kind):
+        def cell(i):
+            return joined(i, lambda s: uz_ref[c, s, :], lambda s: zlo_ref[c, s, :],
+                          lambda s: zhi_ref[c, s, :])
+        def put(i, value):
+            edgez[c, pl.ds(i, ROWS, stride=zvecs), :] = value
+        outer(zvecs, cell, zvec(uz, 0), zvec(pz, 1), kind,
+              lambda j: alz[pl.ds(j * ROWS, ROWS), :],
+              lambda i: accz[c, pl.ds(i, ROWS, stride=zvecs), :], put)
+
+    for_components(3, z_body)
 
     def y_body(c, kind):
         for g in range(groups):
-            def cell(i):
+            base = g * ROWS * width_y
+            def cell(i, g=g, base=base):
                 if HALO <= i < width_y + HALO:
-                    return u_ref[c, pl.ds(g * ROWS * width_y + i - HALO, ROWS, stride=width_y), :]
+                    return u_ref[c, pl.ds(base + i - HALO, ROWS, stride=width_y), :]
                 if i < HALO:
                     return ylo_ref[c, pl.ds(i * planes + g * ROWS, ROWS), :]
                 return yhi_ref[c, pl.ds((i - HALO - width_y) * planes + g * ROWS, ROWS), :]
-            cells = memo(cell)
-            def at(ref):
-                return lambda i: ref[pl.ds(i * planes + g * ROWS, ROWS), :]
-            fluxes = memo(lambda i: flux_of(cells(i), at(uy)(i), lambda: at(py)(i), kind))
-            out = sweep(cells, fluxes, at(aly), 0, width_y)
-            for i in range(width_y):
-                accy[c, pl.ds(g * ROWS * width_y + i, ROWS, stride=width_y), :] = out[i + 1] - out[i]
+            def put(i, value, base=base):
+                edgey[c, pl.ds(base + i, ROWS, stride=width_y), :] = value
+            outer(width_y, cell, yvec(uy, 0, g), yvec(py, 1, g), kind,
+                  lambda j: aly[pl.ds(j * planes + g * ROWS, ROWS), :],
+                  lambda i: accy[c, pl.ds(base + i, ROWS, stride=width_y), :], put)
 
     for_components(2, y_body)
 
-    row = lax.broadcasted_iota(jnp.int32, (ROWS, planes * width_y), 0)
-
-    def z_body(c, kind):
-        def cell(i):
-            value = uz_ref[c, pl.ds(ROWS - HALO + i, ROWS, stride=zvecs), :]
-            if i < HALO:
-                edge = zlo_ref[c, pl.ds(ROWS - HALO + i, 1), :]
-                value = jnp.where(row == 0, edge, value)
-            elif i >= zvecs + HALO:
-                edge = zhi_ref[c, pl.ds(i - zvecs - HALO, 1), :]
-                value = jnp.where(row == ROWS - 1, edge, value)
-            return value
-        cells = memo(cell)
-        fluxes = memo(lambda i: flux_of(cells(i), zvec(uz, i), lambda: zvec(pz, i), kind))
-        out = sweep(cells, fluxes, lambda j: alz[pl.ds(j * ROWS, ROWS), :], 0, zvecs)
-        for i in range(zvecs):
-            accz[c, pl.ds(i, ROWS, stride=zvecs), :] = out[i + 1] - out[i]
-
-    for_components(3, z_body)
+    def between(n, rows, width):
+        position = lax.broadcasted_iota(jnp.int32, (rows, width), 0) % n
+        return (position >= HALO) & (position < n - HALO)
+
+    inside_y = between(width_y, planes * width_y, width_z)
+    inside_z = between(zvecs, width_z, planes * width_y)
 
     def combine(c, _):
-        change = FLUX_FACTOR * (accz[c].T + accx[c] + accy[c])
+        change_z = jnp.where(inside_z, accz[c], edgez[c]).T
+        change_y = jnp.where(inside_y, accy[c], edgey[c])
+        low, high = HALO * ROWS, (planes - HALO) * ROWS
+        change_x = jnp.concatenate([
+            edgex[c, pl.ds(0, low), :], accx[c, pl.ds(low, high - low), :],
+            edgex[c, pl.ds(low, low), :]], axis=0)
+        change = FLUX_FACTOR * (change_x + change_y + change_z)
         if stage == 1:
             value = u_ref[c] + change
         elif stage == 2:
@@ -329,35 +411,28 @@
 
 
 def assemble_kernel(
-    planes, width_y, width_z, place, state_ref, ahead_ref, behind_ref, fresh_ref,
-    u_ref, uz_ref, xlo_ref, xhi_ref, ymsg_lo, ymsg_hi, zmsg_lo, zmsg_hi, joined,
+    planes, width_y, width_z, x_msgs, place, state_ref, ahead_ref, fresh_ref, u_ref, uz_ref, *refs,
 ):
+    refs = list(refs)
+    xmsg_refs = [refs.pop(0) for _ in range(x_msgs)]
+    ymsg_lo, ymsg_hi, zmsg_lo, zmsg_hi, joined = refs
     tube, tubes, shift = place[0], place[1], place[4]
-    tail = behind_ref.shape[1] // ROWS
-    total = tail + planes + ahead_ref.shape[1] // ROWS
+    total = planes + ahead_ref.shape[1] // ROWS
 
     def body(c, _):
-        joined[pl.ds(0, tail * ROWS), :] = behind_ref[c]
-        joined[pl.ds(tail * ROWS, planes * ROWS), :] = state_ref[c]
+        joined[pl.ds(0, planes * ROWS), :] = state_ref[c]
         fresh = fresh_ref[c]
-        for i in range(tail + planes, total):
-            value = ahead_ref[c, pl.ds((i - tail - planes) * ROWS, ROWS), :]
+        for i in range(planes, total):
+            value = ahead_ref[c, pl.ds((i - planes) * ROWS, ROWS), :]
             joined[pl.ds(i * ROWS, ROWS), :] = jnp.where(tube == tubes - 1, fresh, value)
-
-        def plane(i):
-            return joined[pl.ds(pl.multiple_of((tail + shift + i) * ROWS, ROWS), ROWS), :]
-
         for i in range(planes):
-            u_ref[c, pl.ds(i * ROWS, ROWS), :] = plane(i)
-        ground = plane(0)
-        for k in range(HALO):
-            xhi_ref[c, pl.ds(k * ROWS, ROWS), :] = plane(planes + k)
-            xlo_ref[c, pl.ds(k * ROWS, ROWS), :] = jnp.where(tube == 0, ground, plane(k - HALO))
+            u_ref[c, pl.ds(i * ROWS, ROWS), :] = joined[
+                pl.ds(pl.multiple_of((shift + i) * ROWS, ROWS), ROWS), :]
         uz_ref[c, pl.ds(ROWS, width_z), :] = u_ref[c].T
         return 0
 
     lax.fori_loop(0, NCOMP, body, 0)
-    messages(planes, width_y, width_z, place, u_ref, uz_ref, [],
+    messages(planes, width_y, width_z, place, u_ref, uz_ref, xmsg_refs,
              ymsg_lo, ymsg_hi, zmsg_lo, zmsg_hi)
 
 
@@ -468,14 +543,17 @@
     return jax.ShapeDtypeStruct(dims, jnp.float32)
 
 
-def call(kernel, out_shape, scratch, n_in):
+def call(kernel, out_shape, scratch, n_in, scalars=True):
     vmem = pl.BlockSpec(memory_space=pltpu.VMEM)
+    specs = [vmem] * n_in
+    if scalars:
+        specs[0] = pl.BlockSpec(memory_space=pltpu.SMEM)
     return pl.pallas_call(
         kernel,
         out_shape=out_shape,
-        in_specs=[pl.BlockSpec(memory_space=pltpu.SMEM)] + [vmem] * (n_in - 1),
+        in_specs=specs,
         out_specs=jax.tree.map(lambda _: vmem, out_shape),
-        scratch_shapes=scratch,
+        scratch_shapes=[pltpu.VMEM(dims, jnp.float32) for dims in scratch],
         compiler_params=pltpu.CompilerParams(vmem_limit_bytes=48 * 1024 * 1024),
     )
 
@@ -489,6 +567,7 @@
 def on_device(state, fresh, substeps, shift):
     comps, planes, width_y, width_z = state.shape
     cross = planes * width_y
+    zvecs = width_z // ROWS
     tubes = lax.axis_size("tube")
     tube = lax.axis_index("tube")
     swap = tubes == 2
@@ -498,64 +577,59 @@
         tube.astype(jnp.int32), jnp.int32(tubes), jnp.asarray(begins[0], jnp.int32),
         jnp.asarray(begins[1], jnp.int32), shift.astype(jnp.int32)])
 
-    reach = SMAX + HALO
-    flat = state.reshape(comps, cross, width_z)
-    if swap:
-        out = jnp.where(tube == 0, flat[:, cross - reach * width_y:], flat[:, :reach * width_y])
-        ahead = lax.ppermute(out, "tube", [(0, 1), (1, 0)])
-        behind = ahead[:, (reach - 2) * width_y:]
-    else:
-        ahead = moved(flat[:, :reach * width_y], "tube", -1, False)
-        behind = moved(flat[:, cross - 2 * width_y:], "tube", 1, False)
-
     full = shape(comps, cross, width_z)
     fullz = shape(comps, width_z + 2 * ROWS, cross)
     xs = shape(comps, HALO * ROWS, width_z)
     ys = shape(comps, HALO * planes, width_z)
     zs = shape(comps, ROWS, cross)
-    start, uz, xlo, xhi, *msgs = call(
-        functools.partial(assemble_kernel, planes, width_y, width_z),
-        (full, fullz, xs, xs, ys, ys, zs, zs),
-        [pltpu.VMEM(((2 + planes + reach) * ROWS, width_z), jnp.float32)],
-        5,
-    )(place, flat, ahead, behind, fresh)
-
-    def plain(*dims):
-        return pltpu.VMEM(dims, jnp.float32)
-
-    rows_x = (planes + 2 * HALO) * ROWS
-    rows_y = (width_y + 2 * HALO) * planes
-    rows_z = width_z + 2 * ROWS
-    zvecs = width_z // ROWS
-    scratch = (
-        [plain(comps, 2 * HALO * ROWS, width_z)]
-        + [plain(rows_x, width_z)] * 3 + [plain((planes + 1) * ROWS, width_z)]
-        + [plain(rows_y, width_z)] * 3 + [plain((width_y + 1) * planes, width_z)]
-        + [plain(rows_z, cross)] * 3 + [plain((zvecs + 1) * ROWS, cross)]
-        + [plain(3, cross, width_z), plain(comps, cross, width_z), plain(comps, cross, width_z),
-           plain(comps, width_z, cross)]
-    )
+    sent = (full, fullz) + (xs,) * x_msgs + (ys, ys, zs, zs)
+    flat = state.reshape(comps, cross, width_z)
+
+    def shifted(reach):
+        def branch():
+            ahead = moved(flat[:, :reach * width_y], "tube", -1, False)
+            return call(
+                functools.partial(assemble_kernel, planes, width_y, width_z, x_msgs),
+                sent, [((planes + reach) * ROWS, width_z)], 4,
+            )(place, flat, ahead, fresh)
+        return branch
+
+    pieces = 4
+    size = SMAX // pieces
+    start, uz, *msgs = lax.switch(
+        (shift.astype(jnp.int32) - 1) // size, [shifted((n + 1) * size) for n in range(pieces)])
+
+    in_x, in_y, in_z = shape(cross, width_z), shape(cross, width_z), shape(
+        width_z + 2 * ROWS, cross)
+    inner_out = (in_x,) * 3 + (in_y,) * 3 + (in_z,) * 3 + (full, full, shape(comps, width_z, cross))
+    al = [((planes + 1) * ROWS, width_z), ((width_y + 1) * planes, width_z),
+          ((zvecs + 1) * ROWS, cross)]
+    inner_scratch = al + [(3, cross, width_z)]
+    outer_scratch = [
+        (comps, 2 * HALO * ROWS, width_z), (3, 2 * HALO * ROWS, width_z),
+        (3, 2 * HALO * planes, width_z), (3, 2 * ROWS, cross),
+        *al, (comps, 2 * HALO * ROWS, width_z), (comps, cross, width_z), (comps, width_z, cross)]
     current = start
     for stage in (1, 2, 3):
-        ylo = moved(msgs[0], "gy", 1, True)
-        yhi = moved(msgs[1], "gy", -1, True)
-        zlo = moved(msgs[2], "gz", 1, True)
-        zhi = moved(msgs[3], "gz", -1, True)
-        outs = (full,)
+        xmsg, (ylo, yhi, zlo, zhi) = msgs[:x_msgs], msgs[x_msgs:]
+        ylo = moved(ylo, "gy", 1, True)
+        yhi = moved(yhi, "gy", -1, True)
+        if swap:
+            xlo = xhi = lax.ppermute(xmsg[0], "tube", [(0, 1), (1, 0)])
+        else:
+            xhi = moved(xmsg[0], "tube", -1, False)
+            xlo = moved(xmsg[1], "tube", 1, False)
+        zlo = moved(zlo, "gz", 1, True)
+        zhi = moved(zhi, "gz", -1, True)
+        inner = call(
+            functools.partial(inner_kernel, planes, width_y, width_z),
+            inner_out, inner_scratch, 2, False)(current, uz)
+        current, *rest = call(
+            functools.partial(outer_kernel, stage, planes, width_y, width_z, x_msgs),
+            (full,) if stage == 3 else sent, outer_scratch, 11 + len(inner_out),
+        )(place, current, uz, start, fresh, xlo, xhi, ylo, yhi, zlo, zhi, *inner)
         if stage < 3:
-            outs = (full, fullz) + (xs,) * x_msgs + (ys, ys, zs, zs)
-        current, *rest = call(
-            functools.partial(stage_kernel, stage, planes, width_y, width_z, x_msgs),
-            outs, scratch, 11,
-        )(place, current, uz, start, fresh, xlo, xhi, ylo, yhi, zlo, zhi)
-        if stage < 3:
-            uz, *rest = rest
-            msgs = rest[x_msgs:]
-            if swap:
-                xlo = xhi = lax.ppermute(rest[0], "tube", [(0, 1), (1, 0)])
-            else:
-                xhi = moved(rest[0], "tube", -1, False)
-                xlo = moved(rest[1], "tube", 1, False)
+            uz, *msgs = rest
 
     vmem = pl.BlockSpec(memory_space=pltpu.VMEM)
     reacted = pl.pallas_call(

time: 97.7 us -> 96.6 us (0.989)
  waiting for transfers between devices: 25.6 us -> 17.4 us
  Pallas kernels: 46 us -> 52.8 us
  local copies, waits for them, and re-layouts: 1.05 us -> 4.59 us
  starting transfers between devices: 22.5 us -> 20.7 us
  other arithmetic: 1.54 us -> 0 us
    ppermute x3, waiting for transfers between devices: 17.1 us -> 0.01 us  [on_device(): xlo = xhi = lax.ppermute(xmsg[0], 'tube', [(0, 1), (1, 0)])]
    ppermute x12 -> x13, waiting for transfers between devices: 8.55 us -> 17.4 us  [moved(): return lax.ppermute(value, axis, pairs)]
    pallas_call x4 -> x7, Pallas kernels: 43.2 us -> 50 us  [the longest x3 28.7 us: on_device(): call(functools.partial(outer_kernel, stage, planes, width_y, width_z, x_m...]
    ppermute x3, starting transfers between devices: 5.5 us -> 2.03 us  [on_device(): xlo = xhi = lax.ppermute(xmsg[0], 'tube', [(0, 1), (1, 0)])]
    unnamed x8 -> x10, local copies, waits for them, and re-layouts: 0.96 us -> 3.29 us
    ppermute x12 -> x13, starting transfers between devices: 17 us -> 18.7 us  [moved(): return lax.ppermute(value, axis, pairs)]
    select_n x1 -> x0, other arithmetic: 1.54 us -> none  [on_device(): jnp.where(tube == 0, flat[:, cross - reach * width_y:], flat[:, :reach *...]
    slice x1, local copies, waits for them, and re-layouts: 0.01 us -> 1.2 us  [branch(): ahead = moved(flat[:, :reach * width_y], 'tube', -1, False)]
  transfers between devices with their start and end apart: 15 -> 16, of which waited for: 6 -> 1; matrix products, arithmetic and copies ran while one was open for 0% -> 0% of each run, Pallas kernels for 0% -> 19%
where the time goes in v1:
time: 96.6 us; the launch traced here: 96.3 us
  Pallas kernels  52.8 us (55%)
  starting transfers between devices  20.7 us (21%)
  waiting for transfers between devices  17.4 us (18%)
  local copies, waits for them, and re-layouts  4.59 us (5%)
    pallas_call x3, Pallas kernels, on_device(): call(functools.partial(outer_kernel, stage, planes, width_y, width_z, x_m...  28.7 us
    ppermute x13, starting transfers between devices, moved(): return lax.ppermute(value, axis, pairs)  18.7 us
    pallas_call x3, Pallas kernels, on_device(): call(functools.partial(inner_kernel, planes, width_y, width_z), inner_out...  18.6 us
    ppermute x13, waiting for transfers between devices, moved(): return lax.ppermute(value, axis, pairs)  17.4 us
    unnamed x10, local copies, waits for them, and re-layouts  3.29 us
    pallas_call x1, Pallas kernels, branch(): call(functools.partial(assemble_kernel, planes, width_y, width_z, x_msgs)...  2.76 us
    pallas_call x1, Pallas kernels, on_device(): pl.pallas_call(functools.partial(chemistry_kernel, planes, 4), out_shape=...  2.76 us
    ppermute x3, starting transfers between devices, on_device(): xlo = xhi = lax.ppermute(xmsg[0], 'tube', [(0, 1), (1, 0)])  2.03 us
  transfers between devices with their start and end apart: 16, of which 1 were waited for; matrix products, arithmetic and copies ran while one was open for 0% of the time, Pallas kernels for 19%

profile of v1, /device:TPU:0, one launch (start us, length us, event | category | flops | bytes accessed | tf_op | source)
XLA Modules:
  0.0 96.3 jit_solution(16618356927475964423)
XLA Ops:
  0.7 0.1 stack.15.place
  0.8 22.6 %conditional.1 = ((f32[13,128,128]{2,1,0:T(8,128)S(1)}, f32[13,144,128]{2,1,0:T(8,128)S(1)}, f32[13,24,128]{2,1,0:T(8,128)S(1)}, f32[13,48,128]{2,1,0:T(8,128)S(...) conditional(s32[]{:T(128)} %clamp.3, ...), branch_computations={%region_0.1_spmd, %region_1.2_spmd, %region_2.3_spmd, %region_3.4_... | conditional | bytes 7454824 | solution.py:599
  0.8 1.2 %slice.11 = f32[13,96,128]{2,1,0:T(8,128)S(1)} slice(f32[13,128,128]{2,1,0:T(8,128)} %get-tuple-element.39.state_ref), slice={[0:13], [0:96], [0:128]} | slice | bytes 1277952 | tf_op jit(solution)/shard_map/cond/branch_3_fun/slice | solution.py:590
  2.0 1.3 %collective-permute-start.3 = (f32[13,96,128]{2,1,0:T(8,128)S(1)}, f32[13,96,128]{2,1,0:T(8,128)S(1)}, u32[]{:S(2)}, u32[]{:S(2)}) collective-permute-start(f32[13,96,128]{2,1,0:T(8,128)S(1)} %slice.11), channel_id=1, source_target_pairs={{16,0},{17,1},{18,2},{19,3},{20,4},{21,5},{22,6},{23,7},{24,8},{25... | collective-permute-start | bytes 1916936 | tf_op jit(solution)/shard_map/cond/branch_3_fun/ppermute | solution.py:564
  3.3 17.3 %collective-permute-done.3.ahead_ref = f32[13,96,128]{2,1,0:T(8,128)S(1)} collective-permute-done((f32[13,96,128]{2,1,0:T(8,128)S(1)}, f32[13,96,128]{2,1,0:T(8,128)S(1)}, u32[]{:S(2)}, u32[]{:S(2)}) %collective-permute-start.3) | collective-permute-done | bytes 639008 | tf_op jit(solution)/shard_map/cond/branch_3_fun/ppermute | solution.py:564
  20.6 2.8 %branch_3_fun.1 = (f32[13,128,128]{2,1,0:T(8,128)S(1)}, f32[13,144,128]{2,1,0:T(8,128)S(1)}, f32[13,24,128]{2,1,0:T(8,128)S(1)}, f32[13,48,128]{2,1,0:T(8,128)S(...) custom-call(s32[5]{0:T(128)S(1)} %get-tuple-element.38.place, ...), custom_call_target="tpu_custom_call" | custom-call | tf_op jit(solution)/shard_map/cond/branch_3_fun/pallas_call | solution.py:591
  23.4 1.7 %collective-permute-start.6 = (f32[13,48,128]{2,1,0:T(8,128)S(1)}, f32[13,48,128]{2,1,0:T(8,128)S(1)}, u32[]{:S(2)}, u32[]{:S(2)}) collective-permute-start(f32[13,48,128]{2,1,0:T(8,128)S(1)} %get-tuple-element.102), channel_id=1, source_target_pairs={{0,12},{4,0},{8,4},{12,8},{1,13},{5,1},{9,5},{13,9},{2,14},{6,2},{... | collective-permute-start | bytes 958472 | tf_op jit(solution)/shard_map/ppermute | solution.py:564
  25.1 2.4 %collective-permute-start.7 = (f32[13,8,128]{2,1,0:T(8,128)}, f32[13,8,128]{2,1,0:T(8,128)S(1)}, u32[]{:S(2)}, u32[]{:S(2)}) collective-permute-start(f32[13,8,128]{2,1,0:T(8,128)} %get-tuple-element.103), channel_id=1, source_target_pairs={{0,1},{1,2},{2,3},{3,0},{4,5},{5,6},{6,7},{7,4},{8,9},{9,10},{10,1... | collective-permute-start | bytes 159752 | tf_op jit(solution)/shard_map/ppermute | solution.py:564
  27.5 2.0 %collective-permute-start.8 = (f32[13,8,128]{2,1,0:T(8,128)}, f32[13,8,128]{2,1,0:T(8,128)S(1)}, u32[]{:S(2)}, u32[]{:S(2)}) collective-permute-start(f32[13,8,128]{2,1,0:T(8,128)} %get-tuple-element.104), channel_id=1, source_target_pairs={{0,3},{1,0},{2,1},{3,2},{4,7},{5,4},{6,5},{7,6},{8,11},{9,8},{10,9... | collective-permute-start | bytes 159752 | tf_op jit(solution)/shard_map/ppermute | solution.py:564
  29.6 6.2 %shard_map.46 = (f32[128,128]{1,0:T(8,128)S(1)}, f32[128,128]{1,0:T(8,128)S(1)}, f32[128,128]{1,0:T(8,128)S(1)}, f32[128,128]{1,0:T(8,128)S(1)}, f32[128,128]{1,...) custom-call(f32[13,128,128]{2,1,0:T(8,128)S(1)} %get-tuple-element.9, ...), custom_call_target="tpu_custom_call" | custom-call | tf_op jit(solution)/shard_map/pallas_call | solution.py:624
  35.8 0.0 collective-permute-done.7.zlo_ref
  35.8 0.0 collective-permute-done.5.ylo_ref
  35.8 0.0 collective-permute-done.6.yhi_ref
  35.8 9.7 %shard_map.47 = (f32[13,128,128]{2,1,0:T(8,128)S(1)}, f32[13,144,128]{2,1,0:T(8,128)}, f32[13,24,128]{2,1,0:T(8,128)S(1)}, f32[13,48,128]{2,1,0:T(8,128)S(1)}, f...) custom-call(s32[5]{0:T(128)S(1)} %stack.15.place, ...), custom_call_target="tpu_custom_call" | custom-call | tf_op jit(solution)/shard_map/pallas_call | solution.py:627
  45.5 1.8 %collective-permute-start.11 = (f32[13,48,128]{2,1,0:T(8,128)S(1)}, f32[13,48,128]{2,1,0:T(8,128)S(1)}, u32[]{:S(2)}, u32[]{:S(2)}) collective-permute-start(f32[13,48,128]{2,1,0:T(8,128)S(1)} %get-tuple-element.121), channel_id=1, source_target_pairs={{0,12},{4,0},{8,4},{12,8},{1,13},{5,1},{9,5},{13,9},{2,14},{6,2},{... | collective-permute-start | bytes 958472 | tf_op jit(solution)/shard_map/ppermute | solution.py:564
  47.3 2.0 %collective-permute-start.9 = (f32[13,24,128]{2,1,0:T(8,128)S(1)}, f32[13,24,128]{2,1,0:T(8,128)S(1)}, u32[]{:S(2)}, u32[]{:S(2)}) collective-permute-start(f32[13,24,128]{2,1,0:T(8,128)S(1)} %get-tuple-element.119), channel_id=1, source_target_pairs={{0,16},{16,0},{1,17},{17,1},{2,18},{18,2},{3,19},{19,3},{4,20},{20... | collective-permute-start | bytes 479240 | tf_op jit(solution)/shard_map/ppermute | solution.py:618
  49.3 3.8 %collective-permute-start.13 = (f32[13,8,128]{2,1,0:T(8,128)S(1)}, f32[13,8,128]{2,1,0:T(8,128)S(1)}, u32[]{:S(2)}, u32[]{:S(2)}) collective-permute-start(f32[13,8,128]{2,1,0:T(8,128)S(1)} %get-tuple-element.123), channel_id=1, source_target_pairs={{0,3},{1,0},{2,1},{3,2},{4,7},{5,4},{6,5},{7,6},{8,11},{9,8},{10,9... | collective-permute-start | bytes 159752 | tf_op jit(solution)/shard_map/ppermute | solution.py:564
  53.2 1.2 %copy-done = f32[13,144,128]{2,1,0:T(8,128)S(1)} copy-done((f32[13,144,128]{2,1,0:T(8,128)S(1)}, f32[13,144,128]{2,1,0:T(8,128)}, u32[]{:S(2)}) %copy-start) | copy-done | bytes 958488
  54.4 6.2 %shard_map.48 = (f32[128,128]{1,0:T(8,128)S(1)}, f32[128,128]{1,0:T(8,128)S(1)}, f32[128,128]{1,0:T(8,128)S(1)}, f32[128,128]{1,0:T(8,128)S(1)}, f32[128,128]{1,...) custom-call(f32[13,128,128]{2,1,0:T(8,128)S(1)} %get-tuple-element.1, ...), custom_call_target="tpu_custom_call" | custom-call | tf_op jit(solution)/shard_map/pallas_call | solution.py:624
  60.6 0.0 copy-start.2
  60.6 0.9 copy-done.2
  61.5 0.0 collective-permute-done.10.ylo_ref
  61.5 0.0 collective-permute-done.11.yhi_ref
  61.5 10.6 %shard_map.49 = (f32[13,128,128]{2,1,0:T(8,128)S(1)}, f32[13,144,128]{2,1,0:T(8,128)}, f32[13,24,128]{2,1,0:T(8,128)S(1)}, f32[13,48,128]{2,1,0:T(8,128)S(1)}, f...) custom-call(s32[5]{0:T(128)S(1)} %stack.15.place, ...), custom_call_target="tpu_custom_call" | custom-call | tf_op jit(solution)/shard_map/pallas_call | solution.py:627
  72.1 0.0 collective-permute-start.15
  72.1 1.8 %collective-permute-start.16 = (f32[13,48,128]{2,1,0:T(8,128)S(1)}, f32[13,48,128]{2,1,0:T(8,128)S(1)}, u32[]{:S(2)}, u32[]{:S(2)}) collective-permute-start(f32[13,48,128]{2,1,0:T(8,128)S(1)} %get-tuple-element.140), channel_id=1, source_target_pairs={{0,12},{4,0},{8,4},{12,8},{1,13},{5,1},{9,5},{13,9},{2,14},{6,2},{... | collective-permute-start | bytes 958472 | tf_op jit(solution)/shard_map/ppermute | solution.py:564
  73.9 3.8 %collective-permute-start.18 = (f32[13,8,128]{2,1,0:T(8,128)S(1)}, f32[13,8,128]{2,1,0:T(8,128)S(1)}, u32[]{:S(2)}, u32[]{:S(2)}) collective-permute-start(f32[13,8,128]{2,1,0:T(8,128)S(1)} %get-tuple-element.142), channel_id=1, source_target_pairs={{0,3},{1,0},{2,1},{3,2},{4,7},{5,4},{6,5},{7,6},{8,11},{9,8},{10,9... | collective-permute-start | bytes 159752 | tf_op jit(solution)/shard_map/ppermute | solution.py:564
  77.7 1.2 %copy-done.1 = f32[13,144,128]{2,1,0:T(8,128)S(1)} copy-done((f32[13,144,128]{2,1,0:T(8,128)S(1)}, f32[13,144,128]{2,1,0:T(8,128)}, u32[]{:S(2)}) %copy-start.1) | copy-done | bytes 958488
  78.9 6.2 %shard_map.50 = (f32[128,128]{1,0:T(8,128)S(1)}, f32[128,128]{1,0:T(8,128)S(1)}, f32[128,128]{1,0:T(8,128)S(1)}, f32[128,128]{1,0:T(8,128)S(1)}, f32[128,128]{1,...) custom-call(f32[13,128,128]{2,1,0:T(8,128)S(1)} %get-tuple-element.1, ...), custom_call_target="tpu_custom_call" | custom-call | tf_op jit(solution)/shard_map/pallas_call | solution.py:624
  85.1 0.0 copy-start.3
  85.1 8.4 %shard_map.51.third_ref = f32[13,128,128]{2,1,0:T(8,128)S(1)} custom-call(s32[5]{0:T(128)S(1)} %stack.15.place, f32[13,128,128]{2,1,0:T(8,128)S(1)} %get-tuple-element.136.u_ref, f32[13,144,128]{2,1,0:T(8,128)} %get-tuple-element.137.uz_ref, f32[13,128,128]{2,1,0:T(8,128)S(1)} %get-tuple-element.98.u_ref.start_ref, f32[13,8,128]{2,1,0:T(8,128)S(1)} %copy-done.6, ...), custom_call_target="tpu_custom_call" | custom-call | tf_op jit(solution)/shard_map/pallas_call | solution.py:627
  93.5 2.8 %shard_map.52 = f32[13,128,128]{2,1,0:T(8,128)} custom-call(f32[13,128,128]{2,1,0:T(8,128)S(1)} %shard_map.51.third_ref, s32[128,128]{1,0:T(8,128)S(1)} %bitcast.7), custom_call_target="tpu_custom_call" | custom-call | tf_op jit(solution)/shard_map/pallas_call | solution.py:635
  (25 shorter events, 0.1 us)
Async XLA Ops:
  0.8 19.8 %copy-start.5 = (f32[13,128,128]{2,1,0:T(8,128)S(1)}, f32[13,128,128]{2,1,0:T(8,128)}, u32[]{:S(2)}) copy-start(f32[13,128,128]{2,1,0:T(8,128)} %get-tuple-element.39.state_ref) | copy-start | bytes 2555908 | tf_op jit(solution)/shard_map/cond
  0.8 19.8 %copy-start.10 = (f32[13,8,128]{2,1,0:T(8,128)S(1)}, f32[13,8,128]{2,1,0:T(8,128)}, u32[]{:S(2)}) copy-start(f32[13,8,128]{2,1,0:T(8,128)} %get-tuple-element.40.fresh_ref) | copy-start | bytes 159748 | tf_op jit(solution)/shard_map/cond
  2.0 18.6 %collective-permute-start.3 = (f32[13,96,128]{2,1,0:T(8,128)S(1)}, f32[13,96,128]{2,1,0:T(8,128)S(1)}, u32[]{:S(2)}, u32[]{:S(2)}) collective-permute-start(f32[13,96,128]{2,1,0:T(8,128)S(1)} %slice.11), channel_id=1, source_target_pairs={{16,0},{17,1},{18,2},{19,3},{20,4},{21,5},{22,6},{23,7},{24,8},{25... | collective-permute-start | bytes 1916936 | tf_op jit(solution)/shard_map/cond/branch_3_fun/ppermute | solution.py:564
  23.4 12.4 %collective-permute-start.5 = (f32[13,48,128]{2,1,0:T(8,128)S(1)}, f32[13,48,128]{2,1,0:T(8,128)S(1)}, u32[]{:S(2)}, u32[]{:S(2)}) collective-permute-start(f32[13,48,128]{2,1,0:T(8,128)S(1)} %get-tuple-element.101), channel_id=1, source_target_pairs={{0,4},{4,8},{8,12},{12,0},{1,5},{5,9},{9,13},{13,1},{2,6},{6,10},{... | collective-permute-start | bytes 958472 | tf_op jit(solution)/shard_map/ppermute | solution.py:564
  23.4 12.4 %collective-permute-start.6 = (f32[13,48,128]{2,1,0:T(8,128)S(1)}, f32[13,48,128]{2,1,0:T(8,128)S(1)}, u32[]{:S(2)}, u32[]{:S(2)}) collective-permute-start(f32[13,48,128]{2,1,0:T(8,128)S(1)} %get-tuple-element.102), channel_id=1, source_target_pairs={{0,12},{4,0},{8,4},{12,8},{1,13},{5,1},{9,5},{13,9},{2,14},{6,2},{... | collective-permute-start | bytes 958472 | tf_op jit(solution)/shard_map/ppermute | solution.py:564
  25.1 10.7 %collective-permute-start.4 = (f32[13,24,128]{2,1,0:T(8,128)S(1)}, f32[13,24,128]{2,1,0:T(8,128)S(1)}, u32[]{:S(2)}, u32[]{:S(2)}) collective-permute-start(f32[13,24,128]{2,1,0:T(8,128)S(1)} %get-tuple-element.100), channel_id=1, source_target_pairs={{0,16},{16,0},{1,17},{17,1},{2,18},{18,2},{3,19},{19,3},{4,20},{20... | collective-permute-start | bytes 479240 | tf_op jit(solution)/shard_map/ppermute | solution.py:618
  25.1 10.6 %collective-permute-start.7 = (f32[13,8,128]{2,1,0:T(8,128)}, f32[13,8,128]{2,1,0:T(8,128)S(1)}, u32[]{:S(2)}, u32[]{:S(2)}) collective-permute-start(f32[13,8,128]{2,1,0:T(8,128)} %get-tuple-element.103), channel_id=1, source_target_pairs={{0,1},{1,2},{2,3},{3,0},{4,5},{5,6},{6,7},{7,4},{8,9},{9,10},{10,1... | collective-permute-start | bytes 159752 | tf_op jit(solution)/shard_map/ppermute | solution.py:564
  27.5 8.2 %collective-permute-start.8 = (f32[13,8,128]{2,1,0:T(8,128)}, f32[13,8,128]{2,1,0:T(8,128)S(1)}, u32[]{:S(2)}, u32[]{:S(2)}) collective-permute-start(f32[13,8,128]{2,1,0:T(8,128)} %get-tuple-element.104), channel_id=1, source_target_pairs={{0,3},{1,0},{2,1},{3,2},{4,7},{5,4},{6,5},{7,6},{8,11},{9,8},{10,9... | collective-permute-start | bytes 159752 | tf_op jit(solution)/shard_map/ppermute | solution.py:564
  29.6 6.2 %copy-start.6 = (f32[13,8,128]{2,1,0:T(8,128)S(1)}, f32[13,8,128]{2,1,0:T(8,128)}, u32[]{:S(2)}) copy-start(f32[13,8,128]{2,1,0:T(8,128)} %fresh_ref.5) | copy-start | bytes 159748
  45.5 15.9 %collective-permute-start.10 = (f32[13,48,128]{2,1,0:T(8,128)S(1)}, f32[13,48,128]{2,1,0:T(8,128)S(1)}, u32[]{:S(2)}, u32[]{:S(2)}) collective-permute-start(f32[13,48,128]{2,1,0:T(8,128)S(1)} %get-tuple-element.120), channel_id=1, source_target_pairs={{0,4},{4,8},{8,12},{12,0},{1,5},{5,9},{9,13},{13,1},{2,6},{6,10},{... | collective-permute-start | bytes 958472 | tf_op jit(solution)/shard_map/ppermute | solution.py:564
  45.5 15.9 %collective-permute-start.11 = (f32[13,48,128]{2,1,0:T(8,128)S(1)}, f32[13,48,128]{2,1,0:T(8,128)S(1)}, u32[]{:S(2)}, u32[]{:S(2)}) collective-permute-start(f32[13,48,128]{2,1,0:T(8,128)S(1)} %get-tuple-element.121), channel_id=1, source_target_pairs={{0,12},{4,0},{8,4},{12,8},{1,13},{5,1},{9,5},{13,9},{2,14},{6,2},{... | collective-permute-start | bytes 958472 | tf_op jit(solution)/shard_map/ppermute | solution.py:564
  47.3 14.1 %collective-permute-start.9 = (f32[13,24,128]{2,1,0:T(8,128)S(1)}, f32[13,24,128]{2,1,0:T(8,128)S(1)}, u32[]{:S(2)}, u32[]{:S(2)}) collective-permute-start(f32[13,24,128]{2,1,0:T(8,128)S(1)} %get-tuple-element.119), channel_id=1, source_target_pairs={{0,16},{16,0},{1,17},{17,1},{2,18},{18,2},{3,19},{19,3},{4,20},{20... | collective-permute-start | bytes 479240 | tf_op jit(solution)/shard_map/ppermute | solution.py:618
  49.3 12.1 %collective-permute-start.12 = (f32[13,8,128]{2,1,0:T(8,128)S(1)}, f32[13,8,128]{2,1,0:T(8,128)S(1)}, u32[]{:S(2)}, u32[]{:S(2)}) collective-permute-start(f32[13,8,128]{2,1,0:T(8,128)S(1)} %get-tuple-element.122), channel_id=1, source_target_pairs={{0,1},{1,2},{2,3},{3,0},{4,5},{5,6},{6,7},{7,4},{8,9},{9,10},{10,1... | collective-permute-start | bytes 159752 | tf_op jit(solution)/shard_map/ppermute | solution.py:564
  49.3 12.1 %collective-permute-start.13 = (f32[13,8,128]{2,1,0:T(8,128)S(1)}, f32[13,8,128]{2,1,0:T(8,128)S(1)}, u32[]{:S(2)}, u32[]{:S(2)}) collective-permute-start(f32[13,8,128]{2,1,0:T(8,128)S(1)} %get-tuple-element.123), channel_id=1, source_target_pairs={{0,3},{1,0},{2,1},{3,2},{4,7},{5,4},{6,5},{7,6},{8,11},{9,8},{10,9... | collective-permute-start | bytes 159752 | tf_op jit(solution)/shard_map/ppermute | solution.py:564
  53.2 1.2 %copy-start = (f32[13,144,128]{2,1,0:T(8,128)S(1)}, f32[13,144,128]{2,1,0:T(8,128)}, u32[]{:S(2)}) copy-start(f32[13,144,128]{2,1,0:T(8,128)} %get-tuple-element.118.uz_ref) | copy-start | bytes 2875396
  60.6 0.9 copy-start.2
  72.1 13.0 %collective-permute-start.15 = (f32[13,48,128]{2,1,0:T(8,128)S(1)}, f32[13,48,128]{2,1,0:T(8,128)S(1)}, u32[]{:S(2)}, u32[]{:S(2)}) collective-permute-start(f32[13,48,128]{2,1,0:T(8,128)S(1)} %get-tuple-element.139), channel_id=1, source_target_pairs={{0,4},{4,8},{8,12},{12,0},{1,5},{5,9},{9,13},{13,1},{2,6},{6,10},{... | collective-permute-start | bytes 958472 | tf_op jit(solution)/shard_map/ppermute | solution.py:564
  72.1 13.0 %collective-permute-start.16 = (f32[13,48,128]{2,1,0:T(8,128)S(1)}, f32[13,48,128]{2,1,0:T(8,128)S(1)}, u32[]{:S(2)}, u32[]{:S(2)}) collective-permute-start(f32[13,48,128]{2,1,0:T(8,128)S(1)} %get-tuple-element.140), channel_id=1, source_target_pairs={{0,12},{4,0},{8,4},{12,8},{1,13},{5,1},{9,5},{13,9},{2,14},{6,2},{... | collective-permute-start | bytes 958472 | tf_op jit(solution)/shard_map/ppermute | solution.py:564
  73.9 11.2 %collective-permute-start.14 = (f32[13,24,128]{2,1,0:T(8,128)S(1)}, f32[13,24,128]{2,1,0:T(8,128)S(1)}, u32[]{:S(2)}, u32[]{:S(2)}) collective-permute-start(f32[13,24,128]{2,1,0:T(8,128)S(1)} %get-tuple-element.138), channel_id=1, source_target_pairs={{0,16},{16,0},{1,17},{17,1},{2,18},{18,2},{3,19},{19,3},{4,20},{20... | collective-permute-start | bytes 479240 | tf_op jit(solution)/shard_map/ppermute | solution.py:618
  73.9 11.2 %collective-permute-start.17 = (f32[13,8,128]{2,1,0:T(8,128)S(1)}, f32[13,8,128]{2,1,0:T(8,128)S(1)}, u32[]{:S(2)}, u32[]{:S(2)}) collective-permute-start(f32[13,8,128]{2,1,0:T(8,128)S(1)} %get-tuple-element.141), channel_id=1, source_target_pairs={{0,1},{1,2},{2,3},{3,0},{4,5},{5,6},{6,7},{7,4},{8,9},{9,10},{10,1... | collective-permute-start | bytes 159752 | tf_op jit(solution)/shard_map/ppermute | solution.py:564
  73.9 11.2 %collective-permute-start.18 = (f32[13,8,128]{2,1,0:T(8,128)S(1)}, f32[13,8,128]{2,1,0:T(8,128)S(1)}, u32[]{:S(2)}, u32[]{:S(2)}) collective-permute-start(f32[13,8,128]{2,1,0:T(8,128)S(1)} %get-tuple-element.142), channel_id=1, source_target_pairs={{0,3},{1,0},{2,1},{3,2},{4,7},{5,4},{6,5},{7,6},{8,11},{9,8},{10,9... | collective-permute-start | bytes 159752 | tf_op jit(solution)/shard_map/ppermute | solution.py:564
  77.7 1.2 %copy-start.1 = (f32[13,144,128]{2,1,0:T(8,128)S(1)}, f32[13,144,128]{2,1,0:T(8,128)}, u32[]{:S(2)}) copy-start(f32[13,144,128]{2,1,0:T(8,128)} %get-tuple-element.137.uz_ref) | copy-start | bytes 2875396
  85.1 8.4 %copy-start.3 = (s32[16,8,128]{2,1,0:T(8,128)S(1)}, s32[16,8,128]{2,1,0:T(8,128)}, u32[]{:S(2)}) copy-start(s32[16,8,128]{2,1,0:T(8,128)} %param.10) | copy-start | bytes 196612

commit v2 on v1

--- a/solution.py
+++ b/solution.py
@@ -108,14 +108,21 @@
 
 def for_components(dim, body):
     special = 8 + dim
+    generic = NCOMP - 2
+
+    def nth(i):
+        i = jnp.maximum(i, 0)
+        return i + jnp.where(i >= special, 1, 0).astype(jnp.int32)
 
     def step(i, _):
-        body(i + jnp.where(i >= special, 1, 0).astype(jnp.int32), 0)
+        body(nth(i), 0, lambda n: nth(i - n))
         return 0
 
-    lax.fori_loop(0, NCOMP - 2, step, 0)
-    body(special, 1)
-    body(NCOMP - 1, 2)
+    lax.fori_loop(0, generic, step, 0)
+    order = [k for k in range(NCOMP - 1) if k != special] + [special, NCOMP - 1]
+    for turn in (generic, generic + 1):
+        body(order[turn], turn - generic + 1, lambda n, turn=turn: order[turn - n])
+    return order
 
 
 def flux_of(u, speed, pressure, kind):
@@ -127,9 +134,11 @@
 
 
 def own_thermo(planes, width_y, u_ref, x_refs, y_refs, z_refs, tmp):
+    span = planes // 2
+
     def own(i, _):
-        for k in range(2):
-            p = i * 2 + k
+        for k in range(span):
+            p = i * span + k
             here = pl.ds(pl.multiple_of(p * ROWS, ROWS), ROWS)
             u = [u_ref[c, here, :] for c in range(NCOMP)]
             back, pressure, sound = thermo(u)
@@ -144,7 +153,7 @@
                         (x_refs, y_refs)[d][n][where, :] = value
         return 0
 
-    lax.fori_loop(0, planes // 2, own, 0)
+    lax.fori_loop(0, planes // span, own, 0)
     for n in range(3):
         z_refs[n][pl.ds(ROWS, tmp.shape[2]), :] = tmp[n].T
 
@@ -181,7 +190,7 @@
             put(i, out[i + 1] - out[i])
         put(n - HALO, out[n - HALO])
 
-    def x_body(c, kind):
+    def x_body(c, kind, before):
         def put(i, value):
             accx[c, pl.ds(i * ROWS, ROWS), :] = value
         inner(planes, lambda i: u_ref[c, pl.ds((i - HALO) * ROWS, ROWS), :], xvec(ux), xvec(px),
@@ -189,7 +198,7 @@
 
     for_components(1, x_body)
 
-    def z_body(c, kind):
+    def z_body(c, kind, before):
         def put(i, value):
             accz[c, pl.ds(i, ROWS, stride=zvecs), :] = value
         inner(zvecs, lambda i: uz_ref[c, pl.ds(ROWS - HALO + i, ROWS, stride=zvecs), :],
@@ -197,7 +206,7 @@
 
     for_components(3, z_body)
 
-    def y_body(c, kind):
+    def y_body(c, kind, before):
         for g in range(groups):
             def put(i, value, g=g):
                 accy[c, pl.ds(g * ROWS * width_y + i, ROWS, stride=width_y), :] = value
@@ -233,7 +242,7 @@
         newz_ref = refs.pop(0)
         xmsg_refs = [refs.pop(0) for _ in range(x_msgs)]
         ymsg_lo, ymsg_hi, zmsg_lo, zmsg_hi = [refs.pop(0) for _ in range(4)]
-    xh, gx, gy, gz, alx, aly, alz, edgex, edgey, edgez = refs
+    xh, gx, gy, gz, alx, aly, alz, edgex, edgey, edgez, changez = refs
 
     def ghosts(c, _):
         for k in range(HALO):
@@ -255,13 +264,11 @@
     for k in range(2 * HALO):
         ghost_thermo([xh[c, pl.ds(k * ROWS, ROWS), :] for c in range(NCOMP)], 0, gx, k * ROWS)
     for ref, offset in ((ylo_ref, 0), (yhi_ref, HALO)):
-        def ghost_y(k, _, ref=ref, offset=offset):
+        for k in range(HALO):
             for g in range(groups):
-                row = pl.multiple_of(k * planes + g * ROWS, ROWS)
+                row = k * planes + g * ROWS
                 u = [ref[c, pl.ds(row, ROWS), :] for c in range(NCOMP)]
-                ghost_thermo(u, 1, gy, pl.multiple_of(offset * planes + row, ROWS))
-            return 0
-        lax.fori_loop(0, HALO, ghost_y, 0)
+                ghost_thermo(u, 1, gy, offset * planes + row)
     ghost_thermo([zlo_ref[c] for c in range(NCOMP)], 2, gz, 0)
     ghost_thermo([zhi_ref[c] for c in range(NCOMP)], 2, gz, ROWS)
 
@@ -315,7 +322,28 @@
         for i in range(n - HALO, n):
             put(i, out[i + 1] - out[i])
 
-    def x_body(c, kind):
+    def between(n, rows, width):
+        position = lax.broadcasted_iota(jnp.int32, (rows, width), 0) % n
+        return (position >= HALO) & (position < n - HALO)
+
+    inside_y = between(width_y, ROWS, width_z)
+    inside_z = between(zvecs, width_z, planes * width_y)
+
+    def z_body(c, kind, before):
+        def cell(i):
+            return joined(i, lambda s: uz_ref[c, s, :], lambda s: zlo_ref[c, s, :],
+                          lambda s: zhi_ref[c, s, :])
+        def put(i, value):
+            edgez[c, pl.ds(i, ROWS, stride=zvecs), :] = value
+        outer(zvecs, cell, zvec(uz, 0), zvec(pz, 1), kind,
+              lambda j: alz[pl.ds(j * ROWS, ROWS), :],
+              lambda i: accz[c, pl.ds(i, ROWS, stride=zvecs), :], put)
+
+    for_components(3, z_body)
+
+    def x_body(c, kind, before):
+        changez[c] = jnp.where(inside_z, accz[c], edgez[c]).T
+
         def cell(i):
             if HALO <= i < planes + HALO:
                 return u_ref[c, pl.ds((i - HALO) * ROWS, ROWS), :]
@@ -328,19 +356,31 @@
 
     for_components(1, x_body)
 
-    def z_body(c, kind):
-        def cell(i):
-            return joined(i, lambda s: uz_ref[c, s, :], lambda s: zlo_ref[c, s, :],
-                          lambda s: zhi_ref[c, s, :])
-        def put(i, value):
-            edgez[c, pl.ds(i, ROWS, stride=zvecs), :] = value
-        outer(zvecs, cell, zvec(uz, 0), zvec(pz, 1), kind,
-              lambda j: alz[pl.ds(j * ROWS, ROWS), :],
-              lambda i: accz[c, pl.ds(i, ROWS, stride=zvecs), :], put)
-
-    for_components(3, z_body)
-
-    def y_body(c, kind):
+    def update(c):
+        for p in range(planes):
+            here = pl.ds(p * ROWS, ROWS)
+            change = changez[c, here, :] + jnp.where(inside_y, accy[c, here, :], edgey[c, here, :])
+            if HALO <= p < planes - HALO:
+                change = change + accx[c, here, :]
+            else:
+                k = p if p < HALO else p - planes + 2 * HALO
+                change = change + edgex[c, pl.ds(k * ROWS, ROWS), :]
+            value = u_ref[c, here, :] + FLUX_FACTOR * change
+            if stage == 2:
+                value = 0.75 * start_ref[c, here, :] + 0.25 * value
+            elif stage == 3:
+                value = (1.0 / 3.0) * start_ref[c, here, :] + (2.0 / 3.0) * value
+            new_ref[c, here, :] = value
+
+    def pass_on(c):
+        if not last:
+            newz_ref[c, pl.ds(ROWS, width_z), :] = new_ref[c].T
+            messages(c, planes, width_y, width_z, place, new_ref, newz_ref, xmsg_refs,
+                     ymsg_lo, ymsg_hi, zmsg_lo, zmsg_hi)
+
+    def y_body(c, kind, before):
+        pass_on(before(2))
+        update(before(1))
         for g in range(groups):
             base = g * ROWS * width_y
             def cell(i, g=g, base=base):
@@ -355,59 +395,26 @@
                   lambda j: aly[pl.ds(j * planes + g * ROWS, ROWS), :],
                   lambda i: accy[c, pl.ds(base + i, ROWS, stride=width_y), :], put)
 
-    for_components(2, y_body)
-
-    def between(n, rows, width):
-        position = lax.broadcasted_iota(jnp.int32, (rows, width), 0) % n
-        return (position >= HALO) & (position < n - HALO)
-
-    inside_y = between(width_y, planes * width_y, width_z)
-    inside_z = between(zvecs, width_z, planes * width_y)
-
-    def combine(c, _):
-        change_z = jnp.where(inside_z, accz[c], edgez[c]).T
-        change_y = jnp.where(inside_y, accy[c], edgey[c])
-        low, high = HALO * ROWS, (planes - HALO) * ROWS
-        change_x = jnp.concatenate([
-            edgex[c, pl.ds(0, low), :], accx[c, pl.ds(low, high - low), :],
-            edgex[c, pl.ds(low, low), :]], axis=0)
-        change = FLUX_FACTOR * (change_x + change_y + change_z)
-        if stage == 1:
-            value = u_ref[c] + change
-        elif stage == 2:
-            value = 0.75 * start_ref[c] + 0.25 * (u_ref[c] + change)
-        else:
-            value = (1.0 / 3.0) * start_ref[c] + (2.0 / 3.0) * (u_ref[c] + change)
-        new_ref[c] = value
-        if not last:
-            newz_ref[c, pl.ds(ROWS, width_z), :] = value.T
-        return 0
-
-    lax.fori_loop(0, NCOMP, combine, 0)
-    if not last:
-        messages(planes, width_y, width_z, place, new_ref, newz_ref, xmsg_refs,
-                 ymsg_lo, ymsg_hi, zmsg_lo, zmsg_hi)
-
-
-def messages(planes, width_y, width_z, place, u_ref, uz_ref, xmsg_refs, ylo, yhi, zlo, zhi):
-    def body(c, _):
-        for n, ref in enumerate(xmsg_refs):
-            begin = place[2 + n]
-            for k in range(HALO):
-                rows = pl.ds(pl.multiple_of((begin + k) * ROWS, ROWS), ROWS)
-                ref[c, pl.ds(k * ROWS, ROWS), :] = u_ref[c, rows, :]
+    order = for_components(2, y_body)
+    pass_on(order[-2])
+    update(order[-1])
+    pass_on(order[-1])
+
+
+def messages(c, planes, width_y, width_z, place, u_ref, uz_ref, xmsg_refs, ylo, yhi, zlo, zhi):
+    for n, ref in enumerate(xmsg_refs):
+        begin = place[2 + n]
         for k in range(HALO):
-            for g in range(planes // ROWS):
-                there = pl.ds(k * planes + g * ROWS, ROWS)
-                base = g * ROWS * width_y + k
-                yhi[c, there, :] = u_ref[c, pl.ds(base, ROWS, stride=width_y), :]
-                ylo[c, there, :] = u_ref[
-                    c, pl.ds(base + width_y - HALO, ROWS, stride=width_y), :]
-        zhi[c] = uz_ref[c, pl.ds(ROWS, ROWS), :]
-        zlo[c] = uz_ref[c, pl.ds(width_z, ROWS), :]
-        return 0
-
-    lax.fori_loop(0, NCOMP, body, 0)
+            rows = pl.ds(pl.multiple_of((begin + k) * ROWS, ROWS), ROWS)
+            ref[c, pl.ds(k * ROWS, ROWS), :] = u_ref[c, rows, :]
+    for k in range(HALO):
+        for g in range(planes // ROWS):
+            there = pl.ds(k * planes + g * ROWS, ROWS)
+            base = g * ROWS * width_y + k
+            yhi[c, there, :] = u_ref[c, pl.ds(base, ROWS, stride=width_y), :]
+            ylo[c, there, :] = u_ref[c, pl.ds(base + width_y - HALO, ROWS, stride=width_y), :]
+    zhi[c] = uz_ref[c, pl.ds(ROWS, ROWS), :]
+    zlo[c] = uz_ref[c, pl.ds(width_z, ROWS), :]
 
 
 def assemble_kernel(
@@ -415,25 +422,32 @@
 ):
     refs = list(refs)
     xmsg_refs = [refs.pop(0) for _ in range(x_msgs)]
-    ymsg_lo, ymsg_hi, zmsg_lo, zmsg_hi, joined = refs
+    ymsg_lo, ymsg_hi, zmsg_lo, zmsg_hi = refs
     tube, tubes, shift = place[0], place[1], place[4]
-    total = planes + ahead_ref.shape[1] // ROWS
+    reach = ahead_ref.shape[1] // ROWS
+
+    def pass_on(c):
+        uz_ref[c, pl.ds(ROWS, width_z), :] = u_ref[c].T
+        messages(c, planes, width_y, width_z, place, u_ref, uz_ref, xmsg_refs,
+                 ymsg_lo, ymsg_hi, zmsg_lo, zmsg_hi)
 
     def body(c, _):
-        joined[pl.ds(0, planes * ROWS), :] = state_ref[c]
+        pass_on(jnp.maximum(c - 1, 0))
         fresh = fresh_ref[c]
-        for i in range(planes, total):
-            value = ahead_ref[c, pl.ds((i - planes) * ROWS, ROWS), :]
-            joined[pl.ds(i * ROWS, ROWS), :] = jnp.where(tube == tubes - 1, fresh, value)
         for i in range(planes):
-            u_ref[c, pl.ds(i * ROWS, ROWS), :] = joined[
-                pl.ds(pl.multiple_of((shift + i) * ROWS, ROWS), ROWS), :]
-        uz_ref[c, pl.ds(ROWS, width_z), :] = u_ref[c].T
+            source = shift + i
+            own = jnp.minimum(source, planes - 1)
+            value = state_ref[c, pl.ds(pl.multiple_of(own * ROWS, ROWS), ROWS), :]
+            if i >= planes - reach:
+                beyond = jnp.clip(source - planes, 0, reach - 1)
+                other = ahead_ref[c, pl.ds(pl.multiple_of(beyond * ROWS, ROWS), ROWS), :]
+                other = jnp.where(tube == tubes - 1, fresh, other)
+                value = jnp.where(source >= planes, other, value)
+            u_ref[c, pl.ds(i * ROWS, ROWS), :] = value
         return 0
 
     lax.fori_loop(0, NCOMP, body, 0)
-    messages(planes, width_y, width_z, place, u_ref, uz_ref, xmsg_refs,
-             ymsg_lo, ymsg_hi, zmsg_lo, zmsg_hi)
+    pass_on(NCOMP - 1)
 
 
 def powers_of(back):
@@ -554,7 +568,7 @@
         in_specs=specs,
         out_specs=jax.tree.map(lambda _: vmem, out_shape),
         scratch_shapes=[pltpu.VMEM(dims, jnp.float32) for dims in scratch],
-        compiler_params=pltpu.CompilerParams(vmem_limit_bytes=48 * 1024 * 1024),
+        compiler_params=pltpu.CompilerParams(vmem_limit_bytes=16 * 1024 * 1024),
     )
 
 
@@ -590,7 +604,7 @@
             ahead = moved(flat[:, :reach * width_y], "tube", -1, False)
             return call(
                 functools.partial(assemble_kernel, planes, width_y, width_z, x_msgs),
-                sent, [((planes + reach) * ROWS, width_z)], 4,
+                sent, [], 4,
             )(place, flat, ahead, fresh)
         return branch
 
@@ -608,7 +622,8 @@
     outer_scratch = [
         (comps, 2 * HALO * ROWS, width_z), (3, 2 * HALO * ROWS, width_z),
         (3, 2 * HALO * planes, width_z), (3, 2 * ROWS, cross),
-        *al, (comps, 2 * HALO * ROWS, width_z), (comps, cross, width_z), (comps, width_z, cross)]
+        *al, (comps, 2 * HALO * ROWS, width_z), (comps, cross, width_z), (comps, width_z, cross),
+        (comps, cross, width_z)]
     current = start
     for stage in (1, 2, 3):
         xmsg, (ylo, yhi, zlo, zhi) = msgs[:x_msgs], msgs[x_msgs:]
@@ -637,7 +652,7 @@
         out_shape=full,
         in_specs=[vmem, vmem],
         out_specs=vmem,
-        compiler_params=pltpu.CompilerParams(vmem_limit_bytes=48 * 1024 * 1024),
+        compiler_params=pltpu.CompilerParams(vmem_limit_bytes=16 * 1024 * 1024),
     )(current, substeps.reshape(cross, width_z))
     return reacted.reshape(state.shape)
 

time: 96.6 us -> 84.7 us (0.88); the launches traced: 96.3 us -> 86.3 us
  Pallas kernels: 52.8 us -> 46 us
  local copies, waits for them, and re-layouts: 4.59 us -> 1.31 us
    pallas_call x3, Pallas kernels: 28.7 us -> 22.3 us  [on_device(): call(functools.partial(outer_kernel, stage, planes, width_y, width_z, x_m...]
    unnamed x10 -> x4, local copies, waits for them, and re-layouts: 3.29 us -> 0.01 us
  transfers between devices with their start and end apart: 16 -> 16, of which waited for: 1 -> 1; matrix products, arithmetic and copies ran while one was open for 0% -> 0% of each run, Pallas kernels for 19% -> 21%
where the time goes in v2:
time: 84.7 us; the launch traced here: 86.3 us
  Pallas kernels  46 us (54%)
  starting transfers between devices  20.8 us (25%)
  waiting for transfers between devices  17.4 us (21%)
  local copies, waits for them, and re-layouts  1.31 us (2%)
  between operations  0.86 us (1%)
    pallas_call x3, Pallas kernels, on_device(): call(functools.partial(outer_kernel, stage, planes, width_y, width_z, x_m...  22.3 us
    ppermute x13, starting transfers between devices, moved(): return lax.ppermute(value, axis, pairs)  18.7 us
    pallas_call x3, Pallas kernels, on_device(): call(functools.partial(inner_kernel, planes, width_y, width_z), inner_out...  18.3 us
    ppermute x13, waiting for transfers between devices, moved(): return lax.ppermute(value, axis, pairs)  17.4 us
    pallas_call x1, Pallas kernels, on_device(): pl.pallas_call(functools.partial(chemistry_kernel, planes, 4), out_shape=...  2.76 us
    pallas_call x1, Pallas kernels, branch(): call(functools.partial(assemble_kernel, planes, width_y, width_z, x_msgs)...  2.62 us
    ppermute x3, starting transfers between devices, on_device(): xlo = xhi = lax.ppermute(xmsg[0], 'tube', [(0, 1), (1, 0)])  2.03 us
  transfers between devices with their start and end apart: 16, of which 1 were waited for; matrix products, arithmetic and copies ran while one was open for 0% of the time, Pallas kernels for 21%

profile of v2, /device:TPU:0, one launch (start us, length us, event | category | flops | bytes accessed | tf_op | source)
XLA Modules:
  0.0 86.3 jit_solution(10274498764896366372)
XLA Ops:
  0.7 0.1 stack.15.place
  0.8 22.5 %conditional.1 = ((f32[13,128,128]{2,1,0:T(8,128)S(1)}, f32[13,144,128]{2,1,0:T(8,128)S(1)}, f32[13,24,128]{2,1,0:T(8,128)S(1)}, f32[13,48,128]{2,1,0:T(8,128)S(...) conditional(s32[]{:T(128)} %clamp.3, ...), branch_computations={%region_0.1_spmd, %region_1.2_spmd, %region_2.3_spmd, %region_3.4_... | conditional | bytes 7454824 | solution.py:613
  0.8 1.2 %slice.11 = f32[13,96,128]{2,1,0:T(8,128)S(1)} slice(f32[13,128,128]{2,1,0:T(8,128)} %get-tuple-element.39.state_ref), slice={[0:13], [0:96], [0:128]} | slice | bytes 1277952 | tf_op jit(solution)/shard_map/cond/branch_3_fun/slice | solution.py:604
  2.0 1.3 %collective-permute-start.3 = (f32[13,96,128]{2,1,0:T(8,128)S(1)}, f32[13,96,128]{2,1,0:T(8,128)S(1)}, u32[]{:S(2)}, u32[]{:S(2)}) collective-permute-start(f32[13,96,128]{2,1,0:T(8,128)S(1)} %slice.11), channel_id=1, source_target_pairs={{16,0},{17,1},{18,2},{19,3},{20,4},{21,5},{22,6},{23,7},{24,8},{25... | collective-permute-start | bytes 1916936 | tf_op jit(solution)/shard_map/cond/branch_3_fun/ppermute | solution.py:578
  3.3 17.3 %collective-permute-done.3.ahead_ref = f32[13,96,128]{2,1,0:T(8,128)S(1)} collective-permute-done((f32[13,96,128]{2,1,0:T(8,128)S(1)}, f32[13,96,128]{2,1,0:T(8,128)S(1)}, u32[]{:S(2)}, u32[]{:S(2)}) %collective-permute-start.3) | collective-permute-done | bytes 639008 | tf_op jit(solution)/shard_map/cond/branch_3_fun/ppermute | solution.py:578
  20.6 2.6 %branch_3_fun.1 = (f32[13,128,128]{2,1,0:T(8,128)S(1)}, f32[13,144,128]{2,1,0:T(8,128)S(1)}, f32[13,24,128]{2,1,0:T(8,128)S(1)}, f32[13,48,128]{2,1,0:T(8,128)S(...) custom-call(s32[5]{0:T(128)S(1)} %get-tuple-element.38.place, ...), custom_call_target="tpu_custom_call" | custom-call | tf_op jit(solution)/shard_map/cond/branch_3_fun/pallas_call | solution.py:605
  23.2 1.7 %collective-permute-start.6 = (f32[13,48,128]{2,1,0:T(8,128)S(1)}, f32[13,48,128]{2,1,0:T(8,128)S(1)}, u32[]{:S(2)}, u32[]{:S(2)}) collective-permute-start(f32[13,48,128]{2,1,0:T(8,128)S(1)} %get-tuple-element.102), channel_id=1, source_target_pairs={{0,12},{4,0},{8,4},{12,8},{1,13},{5,1},{9,5},{13,9},{2,14},{6,2},{... | collective-permute-start | bytes 958472 | tf_op jit(solution)/shard_map/ppermute | solution.py:578
  25.0 2.4 %collective-permute-start.7 = (f32[13,8,128]{2,1,0:T(8,128)}, f32[13,8,128]{2,1,0:T(8,128)S(1)}, u32[]{:S(2)}, u32[]{:S(2)}) collective-permute-start(f32[13,8,128]{2,1,0:T(8,128)} %get-tuple-element.103), channel_id=1, source_target_pairs={{0,1},{1,2},{2,3},{3,0},{4,5},{5,6},{6,7},{7,4},{8,9},{9,10},{10,1... | collective-permute-start | bytes 159752 | tf_op jit(solution)/shard_map/ppermute | solution.py:578
  27.4 2.0 %collective-permute-start.8 = (f32[13,8,128]{2,1,0:T(8,128)}, f32[13,8,128]{2,1,0:T(8,128)S(1)}, u32[]{:S(2)}, u32[]{:S(2)}) collective-permute-start(f32[13,8,128]{2,1,0:T(8,128)} %get-tuple-element.104), channel_id=1, source_target_pairs={{0,3},{1,0},{2,1},{3,2},{4,7},{5,4},{6,5},{7,6},{8,11},{9,8},{10,9... | collective-permute-start | bytes 159752 | tf_op jit(solution)/shard_map/ppermute | solution.py:578
  29.4 6.1 %shard_map.46 = (f32[128,128]{1,0:T(8,128)S(1)}, f32[128,128]{1,0:T(8,128)S(1)}, f32[128,128]{1,0:T(8,128)S(1)}, f32[128,128]{1,0:T(8,128)S(1)}, f32[128,128]{1,...) custom-call(f32[13,128,128]{2,1,0:T(8,128)S(1)} %get-tuple-element.9, ...), custom_call_target="tpu_custom_call" | custom-call | tf_op jit(solution)/shard_map/pallas_call | solution.py:639
  35.5 0.0 collective-permute-done.7.zlo_ref
  35.5 0.0 collective-permute-done.4.xlo_ref.xhi_ref
  35.6 0.0 collective-permute-done.5.ylo_ref
  35.6 7.5 %shard_map.47 = (f32[13,128,128]{2,1,0:T(8,128)S(1)}, f32[13,144,128]{2,1,0:T(8,128)S(1)}, f32[13,24,128]{2,1,0:T(8,128)S(1)}, f32[13,48,128]{2,1,0:T(8,128)S(1)...) custom-call(s32[5]{0:T(128)S(1)} %stack.15.place, ...), custom_call_target="tpu_custom_call" | custom-call | tf_op jit(solution)/shard_map/pallas_call | solution.py:642
  43.0 0.1 collective-permute-start.10
  43.1 1.8 %collective-permute-start.11 = (f32[13,48,128]{2,1,0:T(8,128)S(1)}, f32[13,48,128]{2,1,0:T(8,128)S(1)}, u32[]{:S(2)}, u32[]{:S(2)}) collective-permute-start(f32[13,48,128]{2,1,0:T(8,128)S(1)} %get-tuple-element.121), channel_id=1, source_target_pairs={{0,12},{4,0},{8,4},{12,8},{1,13},{5,1},{9,5},{13,9},{2,14},{6,2},{... | collective-permute-start | bytes 958472 | tf_op jit(solution)/shard_map/ppermute | solution.py:578
  44.9 2.0 %collective-permute-start.9 = (f32[13,24,128]{2,1,0:T(8,128)S(1)}, f32[13,24,128]{2,1,0:T(8,128)S(1)}, u32[]{:S(2)}, u32[]{:S(2)}) collective-permute-start(f32[13,24,128]{2,1,0:T(8,128)S(1)} %get-tuple-element.119), channel_id=1, source_target_pairs={{0,16},{16,0},{1,17},{17,1},{2,18},{18,2},{3,19},{19,3},{4,20},{20... | collective-permute-start | bytes 479240 | tf_op jit(solution)/shard_map/ppermute | solution.py:633
  46.9 0.0 collective-permute-start.12
  46.9 3.8 %collective-permute-start.13 = (f32[13,8,128]{2,1,0:T(8,128)S(1)}, f32[13,8,128]{2,1,0:T(8,128)S(1)}, u32[]{:S(2)}, u32[]{:S(2)}) collective-permute-start(f32[13,8,128]{2,1,0:T(8,128)S(1)} %get-tuple-element.123), channel_id=1, source_target_pairs={{0,3},{1,0},{2,1},{3,2},{4,7},{5,4},{6,5},{7,6},{8,11},{9,8},{10,9... | collective-permute-start | bytes 159752 | tf_op jit(solution)/shard_map/ppermute | solution.py:578
  50.7 6.1 %shard_map.48 = (f32[128,128]{1,0:T(8,128)S(1)}, f32[128,128]{1,0:T(8,128)S(1)}, f32[128,128]{1,0:T(8,128)S(1)}, f32[128,128]{1,0:T(8,128)S(1)}, f32[128,128]{1,...) custom-call(f32[13,128,128]{2,1,0:T(8,128)S(1)} %get-tuple-element.1, ...), custom_call_target="tpu_custom_call" | custom-call | tf_op jit(solution)/shard_map/pallas_call | solution.py:639
  56.8 0.0 collective-permute-done.12.zlo_ref
  56.8 0.0 collective-permute-done.9.xlo_ref.xhi_ref
  56.8 0.0 collective-permute-done.10.ylo_ref
  56.9 7.6 %shard_map.49 = (f32[13,128,128]{2,1,0:T(8,128)S(1)}, f32[13,144,128]{2,1,0:T(8,128)S(1)}, f32[13,24,128]{2,1,0:T(8,128)S(1)}, f32[13,48,128]{2,1,0:T(8,128)S(1)...) custom-call(s32[5]{0:T(128)S(1)} %stack.15.place, ...), custom_call_target="tpu_custom_call" | custom-call | tf_op jit(solution)/shard_map/pallas_call | solution.py:642
  64.5 0.1 collective-permute-start.15
  64.5 1.7 %collective-permute-start.16 = (f32[13,48,128]{2,1,0:T(8,128)S(1)}, f32[13,48,128]{2,1,0:T(8,128)S(1)}, u32[]{:S(2)}, u32[]{:S(2)}) collective-permute-start(f32[13,48,128]{2,1,0:T(8,128)S(1)} %get-tuple-element.140), channel_id=1, source_target_pairs={{0,12},{4,0},{8,4},{12,8},{1,13},{5,1},{9,5},{13,9},{2,14},{6,2},{... | collective-permute-start | bytes 958472 | tf_op jit(solution)/shard_map/ppermute | solution.py:578
  66.3 0.0 collective-permute-start.14
  66.3 3.8 %collective-permute-start.18 = (f32[13,8,128]{2,1,0:T(8,128)S(1)}, f32[13,8,128]{2,1,0:T(8,128)S(1)}, u32[]{:S(2)}, u32[]{:S(2)}) collective-permute-start(f32[13,8,128]{2,1,0:T(8,128)S(1)} %get-tuple-element.142), channel_id=1, source_target_pairs={{0,3},{1,0},{2,1},{3,2},{4,7},{5,4},{6,5},{7,6},{8,11},{9,8},{10,9... | collective-permute-start | bytes 159752 | tf_op jit(solution)/shard_map/ppermute | solution.py:578
  70.1 6.1 %shard_map.50 = (f32[128,128]{1,0:T(8,128)S(1)}, f32[128,128]{1,0:T(8,128)S(1)}, f32[128,128]{1,0:T(8,128)S(1)}, f32[128,128]{1,0:T(8,128)S(1)}, f32[128,128]{1,...) custom-call(f32[13,128,128]{2,1,0:T(8,128)S(1)} %get-tuple-element.1, ...), custom_call_target="tpu_custom_call" | custom-call | tf_op jit(solution)/shard_map/pallas_call | solution.py:639
  76.3 0.0 copy-start
  76.3 7.2 %shard_map.51.third_ref = f32[13,128,128]{2,1,0:T(8,128)S(1)} custom-call(s32[5]{0:T(128)S(1)} %stack.15.place, f32[13,128,128]{2,1,0:T(8,128)S(1)} %get-tuple-element.136.u_ref, f32[13,144,128]{2,1,0:T(8,128)S(1)} %get-tuple-element.137.uz_ref, f32[13,128,128]{2,1,0:T(8,128)S(1)} %get-tuple-element.98.u_ref.start_ref, f32[13,8,128]{2,1,0:T(8,128)S(1)} %copy-done.3, ...), custom_call_target="tpu_custom_call" | custom-call | tf_op jit(solution)/shard_map/pallas_call | solution.py:642
  83.5 2.8 %shard_map.52 = f32[13,128,128]{2,1,0:T(8,128)} custom-call(f32[13,128,128]{2,1,0:T(8,128)S(1)} %shard_map.51.third_ref, s32[128,128]{1,0:T(8,128)S(1)} %bitcast.7), custom_call_target="tpu_custom_call" | custom-call | tf_op jit(solution)/shard_map/pallas_call | solution.py:650
  (19 shorter events, 0.0 us)
Async XLA Ops:
  0.8 19.8 %copy-start.2 = (f32[13,128,128]{2,1,0:T(8,128)S(1)}, f32[13,128,128]{2,1,0:T(8,128)}, u32[]{:S(2)}) copy-start(f32[13,128,128]{2,1,0:T(8,128)} %get-tuple-element.39.state_ref) | copy-start | bytes 2555908 | tf_op jit(solution)/shard_map/cond
  0.8 19.8 %copy-start.7 = (f32[13,8,128]{2,1,0:T(8,128)S(1)}, f32[13,8,128]{2,1,0:T(8,128)}, u32[]{:S(2)}) copy-start(f32[13,8,128]{2,1,0:T(8,128)} %get-tuple-element.40.fresh_ref) | copy-start | bytes 159748 | tf_op jit(solution)/shard_map/cond
  2.0 18.6 %collective-permute-start.3 = (f32[13,96,128]{2,1,0:T(8,128)S(1)}, f32[13,96,128]{2,1,0:T(8,128)S(1)}, u32[]{:S(2)}, u32[]{:S(2)}) collective-permute-start(f32[13,96,128]{2,1,0:T(8,128)S(1)} %slice.11), channel_id=1, source_target_pairs={{16,0},{17,1},{18,2},{19,3},{20,4},{21,5},{22,6},{23,7},{24,8},{25... | collective-permute-start | bytes 1916936 | tf_op jit(solution)/shard_map/cond/branch_3_fun/ppermute | solution.py:578
  23.2 12.3 %collective-permute-start.5 = (f32[13,48,128]{2,1,0:T(8,128)S(1)}, f32[13,48,128]{2,1,0:T(8,128)S(1)}, u32[]{:S(2)}, u32[]{:S(2)}) collective-permute-start(f32[13,48,128]{2,1,0:T(8,128)S(1)} %get-tuple-element.101), channel_id=1, source_target_pairs={{0,4},{4,8},{8,12},{12,0},{1,5},{5,9},{9,13},{13,1},{2,6},{6,10},{... | collective-permute-start | bytes 958472 | tf_op jit(solution)/shard_map/ppermute | solution.py:578
  23.2 12.3 %collective-permute-start.6 = (f32[13,48,128]{2,1,0:T(8,128)S(1)}, f32[13,48,128]{2,1,0:T(8,128)S(1)}, u32[]{:S(2)}, u32[]{:S(2)}) collective-permute-start(f32[13,48,128]{2,1,0:T(8,128)S(1)} %get-tuple-element.102), channel_id=1, source_target_pairs={{0,12},{4,0},{8,4},{12,8},{1,13},{5,1},{9,5},{13,9},{2,14},{6,2},{... | collective-permute-start | bytes 958472 | tf_op jit(solution)/shard_map/ppermute | solution.py:578
  25.0 10.6 %collective-permute-start.4 = (f32[13,24,128]{2,1,0:T(8,128)S(1)}, f32[13,24,128]{2,1,0:T(8,128)S(1)}, u32[]{:S(2)}, u32[]{:S(2)}) collective-permute-start(f32[13,24,128]{2,1,0:T(8,128)S(1)} %get-tuple-element.100), channel_id=1, source_target_pairs={{0,16},{16,0},{1,17},{17,1},{2,18},{18,2},{3,19},{19,3},{4,20},{20... | collective-permute-start | bytes 479240 | tf_op jit(solution)/shard_map/ppermute | solution.py:633
  25.0 10.5 %collective-permute-start.7 = (f32[13,8,128]{2,1,0:T(8,128)}, f32[13,8,128]{2,1,0:T(8,128)S(1)}, u32[]{:S(2)}, u32[]{:S(2)}) collective-permute-start(f32[13,8,128]{2,1,0:T(8,128)} %get-tuple-element.103), channel_id=1, source_target_pairs={{0,1},{1,2},{2,3},{3,0},{4,5},{5,6},{6,7},{7,4},{8,9},{9,10},{10,1... | collective-permute-start | bytes 159752 | tf_op jit(solution)/shard_map/ppermute | solution.py:578
  27.4 8.1 %collective-permute-start.8 = (f32[13,8,128]{2,1,0:T(8,128)}, f32[13,8,128]{2,1,0:T(8,128)S(1)}, u32[]{:S(2)}, u32[]{:S(2)}) collective-permute-start(f32[13,8,128]{2,1,0:T(8,128)} %get-tuple-element.104), channel_id=1, source_target_pairs={{0,3},{1,0},{2,1},{3,2},{4,7},{5,4},{6,5},{7,6},{8,11},{9,8},{10,9... | collective-permute-start | bytes 159752 | tf_op jit(solution)/shard_map/ppermute | solution.py:578
  29.4 6.2 %copy-start.3 = (f32[13,8,128]{2,1,0:T(8,128)S(1)}, f32[13,8,128]{2,1,0:T(8,128)}, u32[]{:S(2)}) copy-start(f32[13,8,128]{2,1,0:T(8,128)} %fresh_ref.5) | copy-start | bytes 159748
  43.0 13.8 %collective-permute-start.10 = (f32[13,48,128]{2,1,0:T(8,128)S(1)}, f32[13,48,128]{2,1,0:T(8,128)S(1)}, u32[]{:S(2)}, u32[]{:S(2)}) collective-permute-start(f32[13,48,128]{2,1,0:T(8,128)S(1)} %get-tuple-element.120), channel_id=1, source_target_pairs={{0,4},{4,8},{8,12},{12,0},{1,5},{5,9},{9,13},{13,1},{2,6},{6,10},{... | collective-permute-start | bytes 958472 | tf_op jit(solution)/shard_map/ppermute | solution.py:578
  43.1 13.7 %collective-permute-start.11 = (f32[13,48,128]{2,1,0:T(8,128)S(1)}, f32[13,48,128]{2,1,0:T(8,128)S(1)}, u32[]{:S(2)}, u32[]{:S(2)}) collective-permute-start(f32[13,48,128]{2,1,0:T(8,128)S(1)} %get-tuple-element.121), channel_id=1, source_target_pairs={{0,12},{4,0},{8,4},{12,8},{1,13},{5,1},{9,5},{13,9},{2,14},{6,2},{... | collective-permute-start | bytes 958472 | tf_op jit(solution)/shard_map/ppermute | solution.py:578
  44.9 12.0 %collective-permute-start.9 = (f32[13,24,128]{2,1,0:T(8,128)S(1)}, f32[13,24,128]{2,1,0:T(8,128)S(1)}, u32[]{:S(2)}, u32[]{:S(2)}) collective-permute-start(f32[13,24,128]{2,1,0:T(8,128)S(1)} %get-tuple-element.119), channel_id=1, source_target_pairs={{0,16},{16,0},{1,17},{17,1},{2,18},{18,2},{3,19},{19,3},{4,20},{20... | collective-permute-start | bytes 479240 | tf_op jit(solution)/shard_map/ppermute | solution.py:633
  46.9 9.9 %collective-permute-start.12 = (f32[13,8,128]{2,1,0:T(8,128)S(1)}, f32[13,8,128]{2,1,0:T(8,128)S(1)}, u32[]{:S(2)}, u32[]{:S(2)}) collective-permute-start(f32[13,8,128]{2,1,0:T(8,128)S(1)} %get-tuple-element.122), channel_id=1, source_target_pairs={{0,1},{1,2},{2,3},{3,0},{4,5},{5,6},{6,7},{7,4},{8,9},{9,10},{10,1... | collective-permute-start | bytes 159752 | tf_op jit(solution)/shard_map/ppermute | solution.py:578
  46.9 9.9 %collective-permute-start.13 = (f32[13,8,128]{2,1,0:T(8,128)S(1)}, f32[13,8,128]{2,1,0:T(8,128)S(1)}, u32[]{:S(2)}, u32[]{:S(2)}) collective-permute-start(f32[13,8,128]{2,1,0:T(8,128)S(1)} %get-tuple-element.123), channel_id=1, source_target_pairs={{0,3},{1,0},{2,1},{3,2},{4,7},{5,4},{6,5},{7,6},{8,11},{9,8},{10,9... | collective-permute-start | bytes 159752 | tf_op jit(solution)/shard_map/ppermute | solution.py:578
  64.5 11.8 %collective-permute-start.15 = (f32[13,48,128]{2,1,0:T(8,128)S(1)}, f32[13,48,128]{2,1,0:T(8,128)S(1)}, u32[]{:S(2)}, u32[]{:S(2)}) collective-permute-start(f32[13,48,128]{2,1,0:T(8,128)S(1)} %get-tuple-element.139), channel_id=1, source_target_pairs={{0,4},{4,8},{8,12},{12,0},{1,5},{5,9},{9,13},{13,1},{2,6},{6,10},{... | collective-permute-start | bytes 958472 | tf_op jit(solution)/shard_map/ppermute | solution.py:578
  64.5 11.7 %collective-permute-start.16 = (f32[13,48,128]{2,1,0:T(8,128)S(1)}, f32[13,48,128]{2,1,0:T(8,128)S(1)}, u32[]{:S(2)}, u32[]{:S(2)}) collective-permute-start(f32[13,48,128]{2,1,0:T(8,128)S(1)} %get-tuple-element.140), channel_id=1, source_target_pairs={{0,12},{4,0},{8,4},{12,8},{1,13},{5,1},{9,5},{13,9},{2,14},{6,2},{... | collective-permute-start | bytes 958472 | tf_op jit(solution)/shard_map/ppermute | solution.py:578
  66.3 10.0 %collective-permute-start.14 = (f32[13,24,128]{2,1,0:T(8,128)S(1)}, f32[13,24,128]{2,1,0:T(8,128)S(1)}, u32[]{:S(2)}, u32[]{:S(2)}) collective-permute-start(f32[13,24,128]{2,1,0:T(8,128)S(1)} %get-tuple-element.138), channel_id=1, source_target_pairs={{0,16},{16,0},{1,17},{17,1},{2,18},{18,2},{3,19},{19,3},{4,20},{20... | collective-permute-start | bytes 479240 | tf_op jit(solution)/shard_map/ppermute | solution.py:633
  66.3 9.9 %collective-permute-start.17 = (f32[13,8,128]{2,1,0:T(8,128)S(1)}, f32[13,8,128]{2,1,0:T(8,128)S(1)}, u32[]{:S(2)}, u32[]{:S(2)}) collective-permute-start(f32[13,8,128]{2,1,0:T(8,128)S(1)} %get-tuple-element.141), channel_id=1, source_target_pairs={{0,1},{1,2},{2,3},{3,0},{4,5},{5,6},{6,7},{7,4},{8,9},{9,10},{10,1... | collective-permute-start | bytes 159752 | tf_op jit(solution)/shard_map/ppermute | solution.py:578
  66.3 9.9 %collective-permute-start.18 = (f32[13,8,128]{2,1,0:T(8,128)S(1)}, f32[13,8,128]{2,1,0:T(8,128)S(1)}, u32[]{:S(2)}, u32[]{:S(2)}) collective-permute-start(f32[13,8,128]{2,1,0:T(8,128)S(1)} %get-tuple-element.142), channel_id=1, source_target_pairs={{0,3},{1,0},{2,1},{3,2},{4,7},{5,4},{6,5},{7,6},{8,11},{9,8},{10,9... | collective-permute-start | bytes 159752 | tf_op jit(solution)/shard_map/ppermute | solution.py:578
  76.3 7.2 %copy-start = (s32[16,8,128]{2,1,0:T(8,128)S(1)}, s32[16,8,128]{2,1,0:T(8,128)}, u32[]{:S(2)}) copy-start(s32[16,8,128]{2,1,0:T(8,128)} %param.10) | copy-start | bytes 196612

commit v3 on v2

--- a/solution.py
+++ b/solution.py
@@ -106,23 +106,15 @@
     return back, pressure, sound
 
 
-def for_components(dim, body):
-    special = 8 + dim
-    generic = NCOMP - 2
-
-    def nth(i):
-        i = jnp.maximum(i, 0)
-        return i + jnp.where(i >= special, 1, 0).astype(jnp.int32)
-
-    def step(i, _):
-        body(nth(i), 0, lambda n: nth(i - n))
+def for_components(body):
+    def step(c, _):
+        body(c, (0, 0, 0), lambda n: jnp.maximum(c - n, 0))
         return 0
 
-    lax.fori_loop(0, generic, step, 0)
-    order = [k for k in range(NCOMP - 1) if k != special] + [special, NCOMP - 1]
-    for turn in (generic, generic + 1):
-        body(order[turn], turn - generic + 1, lambda n, turn=turn: order[turn - n])
-    return order
+    lax.fori_loop(0, 9, step, 0)
+    kinds = [(1, 0, 0), (0, 1, 0), (0, 0, 1), (2, 2, 2)]
+    for c in range(9, NCOMP):
+        body(c, kinds[c - 9], lambda n, c=c: c - n)
 
 
 def flux_of(u, speed, pressure, kind):
@@ -190,23 +182,19 @@
             put(i, out[i + 1] - out[i])
         put(n - HALO, out[n - HALO])
 
-    def x_body(c, kind, before):
+    def x_body(c, kind):
         def put(i, value):
             accx[c, pl.ds(i * ROWS, ROWS), :] = value
         inner(planes, lambda i: u_ref[c, pl.ds((i - HALO) * ROWS, ROWS), :], xvec(ux), xvec(px),
               kind, lambda j: alx[pl.ds(j * ROWS, ROWS), :], put)
 
-    for_components(1, x_body)
-
-    def z_body(c, kind, before):
+    def z_body(c, kind):
         def put(i, value):
             accz[c, pl.ds(i, ROWS, stride=zvecs), :] = value
         inner(zvecs, lambda i: uz_ref[c, pl.ds(ROWS - HALO + i, ROWS, stride=zvecs), :],
               zvec(uz), zvec(pz), kind, lambda j: alz[pl.ds(j * ROWS, ROWS), :], put)
 
-    for_components(3, z_body)
-
-    def y_body(c, kind, before):
+    def y_body(c, kind):
         for g in range(groups):
             def put(i, value, g=g):
                 accy[c, pl.ds(g * ROWS * width_y + i, ROWS, stride=width_y), :] = value
@@ -215,7 +203,12 @@
             inner(width_y, cell, yvec(uy, g), yvec(py, g), kind,
                   lambda j: aly[pl.ds(j * planes + g * ROWS, ROWS), :], put)
 
-    for_components(2, y_body)
+    def body(c, kinds, before):
+        x_body(c, kinds[0])
+        z_body(c, kinds[2])
+        y_body(c, kinds[1])
+
+    for_components(body)
 
 
 def largest(speed, faces, ref, place):
@@ -329,7 +322,7 @@
     inside_y = between(width_y, ROWS, width_z)
     inside_z = between(zvecs, width_z, planes * width_y)
 
-    def z_body(c, kind, before):
+    def z_body(c, kind):
         def cell(i):
             return joined(i, lambda s: uz_ref[c, s, :], lambda s: zlo_ref[c, s, :],
                           lambda s: zhi_ref[c, s, :])
@@ -339,11 +332,7 @@
               lambda j: alz[pl.ds(j * ROWS, ROWS), :],
               lambda i: accz[c, pl.ds(i, ROWS, stride=zvecs), :], put)
 
-    for_components(3, z_body)
-
-    def x_body(c, kind, before):
-        changez[c] = jnp.where(inside_z, accz[c], edgez[c]).T
-
+    def x_body(c, kind):
         def cell(i):
             if HALO <= i < planes + HALO:
                 return u_ref[c, pl.ds((i - HALO) * ROWS, ROWS), :]
@@ -354,12 +343,11 @@
               lambda j: alx[pl.ds(j * ROWS, ROWS), :],
               lambda i: accx[c, pl.ds(i * ROWS, ROWS), :], put)
 
-    for_components(1, x_body)
-
     def update(c):
+        changez[...] = jnp.where(inside_z, accz[c], edgez[c]).T
         for p in range(planes):
             here = pl.ds(p * ROWS, ROWS)
-            change = changez[c, here, :] + jnp.where(inside_y, accy[c, here, :], edgey[c, here, :])
+            change = changez[here, :] + jnp.where(inside_y, accy[c, here, :], edgey[c, here, :])
             if HALO <= p < planes - HALO:
                 change = change + accx[c, here, :]
             else:
@@ -378,9 +366,7 @@
             messages(c, planes, width_y, width_z, place, new_ref, newz_ref, xmsg_refs,
                      ymsg_lo, ymsg_hi, zmsg_lo, zmsg_hi)
 
-    def y_body(c, kind, before):
-        pass_on(before(2))
-        update(before(1))
+    def y_body(c, kind):
         for g in range(groups):
             base = g * ROWS * width_y
             def cell(i, g=g, base=base):
@@ -395,10 +381,17 @@
                   lambda j: aly[pl.ds(j * planes + g * ROWS, ROWS), :],
                   lambda i: accy[c, pl.ds(base + i, ROWS, stride=width_y), :], put)
 
-    order = for_components(2, y_body)
-    pass_on(order[-2])
-    update(order[-1])
-    pass_on(order[-1])
+    def body(c, kinds, before):
+        pass_on(before(2))
+        update(before(1))
+        z_body(c, kinds[2])
+        x_body(c, kinds[0])
+        y_body(c, kinds[1])
+
+    for_components(body)
+    pass_on(NCOMP - 2)
+    update(NCOMP - 1)
+    pass_on(NCOMP - 1)
 
 
 def messages(c, planes, width_y, width_z, place, u_ref, uz_ref, xmsg_refs, ylo, yhi, zlo, zhi):
@@ -431,8 +424,9 @@
         messages(c, planes, width_y, width_z, place, u_ref, uz_ref, xmsg_refs,
                  ymsg_lo, ymsg_hi, zmsg_lo, zmsg_hi)
 
-    def body(c, _):
-        pass_on(jnp.maximum(c - 1, 0))
+    for c in range(NCOMP):
+        if c:
+            pass_on(c - 1)
         fresh = fresh_ref[c]
         for i in range(planes):
             source = shift + i
@@ -444,9 +438,6 @@
                 other = jnp.where(tube == tubes - 1, fresh, other)
                 value = jnp.where(source >= planes, other, value)
             u_ref[c, pl.ds(i * ROWS, ROWS), :] = value
-        return 0
-
-    lax.fori_loop(0, NCOMP, body, 0)
     pass_on(NCOMP - 1)
 
 
@@ -623,7 +614,7 @@
         (comps, 2 * HALO * ROWS, width_z), (3, 2 * HALO * ROWS, width_z),
         (3, 2 * HALO * planes, width_z), (3, 2 * ROWS, cross),
         *al, (comps, 2 * HALO * ROWS, width_z), (comps, cross, width_z), (comps, width_z, cross),
-        (comps, cross, width_z)]
+        (cross, width_z)]
     current = start
     for stage in (1, 2, 3):
         xmsg, (ylo, yhi, zlo, zhi) = msgs[:x_msgs], msgs[x_msgs:]

time: 84.7 us -> 76.8 us (0.907); the launches traced: 86.3 us -> 76.6 us
  Pallas kernels: 46 us -> 39.8 us
  waiting for transfers between devices: 17.4 us -> 13.9 us
    pallas_call x3, Pallas kernels: 22.3 us -> 18.6 us  [on_device(): call(functools.partial(outer_kernel, stage, planes, width_y, width_z, x_m...]
    ppermute x13, waiting for transfers between devices: 17.4 us -> 13.9 us  [moved(): return lax.ppermute(value, axis, pairs)]
    pallas_call x3, Pallas kernels: 18.3 us -> 16.8 us  [on_device(): call(functools.partial(inner_kernel, planes, width_y, width_z), inner_out...]
    pallas_call x1, Pallas kernels: 2.62 us -> 1.69 us  [branch(): call(functools.partial(assemble_kernel, planes, width_y, width_z, x_msgs)...]
  transfers between devices with their start and end apart: 16 -> 16, of which waited for: 1 -> 1; matrix products, arithmetic and copies ran while one was open for 0% -> 0% of each run, Pallas kernels for 21% -> 22%
where the time goes in v3:
time: 76.8 us; the launch traced here: 76.6 us
  Pallas kernels  39.8 us (52%)
  starting transfers between devices  20.8 us (27%)
  waiting for transfers between devices  13.9 us (18%)
  local copies, waits for them, and re-layouts  1.24 us (2%)
  between operations  0.87 us (1%)
    ppermute x13, starting transfers between devices, moved(): return lax.ppermute(value, axis, pairs)  18.7 us
    pallas_call x3, Pallas kernels, on_device(): call(functools.partial(outer_kernel, stage, planes, width_y, width_z, x_m...  18.6 us
    pallas_call x3, Pallas kernels, on_device(): call(functools.partial(inner_kernel, planes, width_y, width_z), inner_out...  16.8 us
    ppermute x13, waiting for transfers between devices, moved(): return lax.ppermute(value, axis, pairs)  13.9 us
    pallas_call x1, Pallas kernels, on_device(): pl.pallas_call(functools.partial(chemistry_kernel, planes, 4), out_shape=...  2.76 us
    ppermute x3, starting transfers between devices, on_device(): xlo = xhi = lax.ppermute(xmsg[0], 'tube', [(0, 1), (1, 0)])  2.03 us
    pallas_call x1, Pallas kernels, branch(): call(functools.partial(assemble_kernel, planes, width_y, width_z, x_msgs)...  1.69 us
  transfers between devices with their start and end apart: 16, of which 1 were waited for; matrix products, arithmetic and copies ran while one was open for 0% of the time, Pallas kernels for 22%

profile of v3, /device:TPU:0, one launch (start us, length us, event | category | flops | bytes accessed | tf_op | source)
XLA Modules:
  0.0 76.6 jit_solution(4577412149626528529)
XLA Ops:
  0.7 0.1 stack.15.place
  0.8 18.0 %conditional.1 = ((f32[13,128,128]{2,1,0:T(8,128)S(1)}, f32[13,144,128]{2,1,0:T(8,128)S(1)}, f32[13,24,128]{2,1,0:T(8,128)S(1)}, f32[13,48,128]{2,1,0:T(8,128)S(...) conditional(s32[]{:T(128)} %clamp.3, ...), branch_computations={%region_0.1_spmd, %region_1.2_spmd, %region_2.3_spmd, %region_3.4_... | conditional | bytes 7454824 | solution.py:604
  0.8 1.1 %slice.10 = f32[13,72,128]{2,1,0:T(8,128)S(1)} slice(f32[13,128,128]{2,1,0:T(8,128)} %get-tuple-element.36.state_ref), slice={[0:13], [0:72], [0:128]} | slice | bytes 958464 | tf_op jit(solution)/shard_map/cond/branch_2_fun/slice | solution.py:595
  1.9 1.3 %collective-permute-start.2 = (f32[13,72,128]{2,1,0:T(8,128)S(1)}, f32[13,72,128]{2,1,0:T(8,128)S(1)}, u32[]{:S(2)}, u32[]{:S(2)}) collective-permute-start(f32[13,72,128]{2,1,0:T(8,128)S(1)} %slice.10), channel_id=1, source_target_pairs={{16,0},{17,1},{18,2},{19,3},{20,4},{21,5},{22,6},{23,7},{24,8},{25... | collective-permute-start | bytes 1437704 | tf_op jit(solution)/shard_map/cond/branch_2_fun/ppermute | solution.py:569
  3.2 13.9 %collective-permute-done.2.ahead_ref = f32[13,72,128]{2,1,0:T(8,128)S(1)} collective-permute-done((f32[13,72,128]{2,1,0:T(8,128)S(1)}, f32[13,72,128]{2,1,0:T(8,128)S(1)}, u32[]{:S(2)}, u32[]{:S(2)}) %collective-permute-start.2) | collective-permute-done | bytes 479264 | tf_op jit(solution)/shard_map/cond/branch_2_fun/ppermute | solution.py:569
  17.1 1.7 %branch_2_fun.1 = (f32[13,128,128]{2,1,0:T(8,128)S(1)}, f32[13,144,128]{2,1,0:T(8,128)S(1)}, f32[13,24,128]{2,1,0:T(8,128)S(1)}, f32[13,48,128]{2,1,0:T(8,128)S(...) custom-call(s32[5]{0:T(128)S(1)} %get-tuple-element.35.place, ...), custom_call_target="tpu_custom_call" | custom-call | tf_op jit(solution)/shard_map/cond/branch_2_fun/pallas_call | solution.py:596
  18.8 1.7 %collective-permute-start.6 = (f32[13,48,128]{2,1,0:T(8,128)S(1)}, f32[13,48,128]{2,1,0:T(8,128)S(1)}, u32[]{:S(2)}, u32[]{:S(2)}) collective-permute-start(f32[13,48,128]{2,1,0:T(8,128)S(1)} %get-tuple-element.102), channel_id=1, source_target_pairs={{0,12},{4,0},{8,4},{12,8},{1,13},{5,1},{9,5},{13,9},{2,14},{6,2},{... | collective-permute-start | bytes 958472 | tf_op jit(solution)/shard_map/ppermute | solution.py:569
  20.6 2.4 %collective-permute-start.7 = (f32[13,8,128]{2,1,0:T(8,128)}, f32[13,8,128]{2,1,0:T(8,128)S(1)}, u32[]{:S(2)}, u32[]{:S(2)}) collective-permute-start(f32[13,8,128]{2,1,0:T(8,128)} %get-tuple-element.103), channel_id=1, source_target_pairs={{0,1},{1,2},{2,3},{3,0},{4,5},{5,6},{6,7},{7,4},{8,9},{9,10},{10,1... | collective-permute-start | bytes 159752 | tf_op jit(solution)/shard_map/ppermute | solution.py:569
  23.0 2.0 %collective-permute-start.8 = (f32[13,8,128]{2,1,0:T(8,128)}, f32[13,8,128]{2,1,0:T(8,128)S(1)}, u32[]{:S(2)}, u32[]{:S(2)}) collective-permute-start(f32[13,8,128]{2,1,0:T(8,128)} %get-tuple-element.104), channel_id=1, source_target_pairs={{0,3},{1,0},{2,1},{3,2},{4,7},{5,4},{6,5},{7,6},{8,11},{9,8},{10,9... | collective-permute-start | bytes 159752 | tf_op jit(solution)/shard_map/ppermute | solution.py:569
  25.0 5.6 %shard_map.46 = (f32[128,128]{1,0:T(8,128)S(1)}, f32[128,128]{1,0:T(8,128)S(1)}, f32[128,128]{1,0:T(8,128)S(1)}, f32[128,128]{1,0:T(8,128)S(1)}, f32[128,128]{1,...) custom-call(f32[13,128,128]{2,1,0:T(8,128)S(1)} %get-tuple-element.9, ...), custom_call_target="tpu_custom_call" | custom-call | tf_op jit(solution)/shard_map/pallas_call | solution.py:630
  30.6 0.0 collective-permute-done.8.zhi_ref
  30.6 0.0 collective-permute-done.4.xlo_ref.xhi_ref
  30.6 0.0 collective-permute-done.6.yhi_ref
  30.6 6.1 %shard_map.47 = (f32[13,128,128]{2,1,0:T(8,128)S(1)}, f32[13,144,128]{2,1,0:T(8,128)S(1)}, f32[13,24,128]{2,1,0:T(8,128)S(1)}, f32[13,48,128]{2,1,0:T(8,128)S(1)...) custom-call(s32[5]{0:T(128)S(1)} %stack.15.place, ...), custom_call_target="tpu_custom_call" | custom-call | tf_op jit(solution)/shard_map/pallas_call | solution.py:633
  36.8 0.1 collective-permute-start.10
  36.9 1.8 %collective-permute-start.11 = (f32[13,48,128]{2,1,0:T(8,128)S(1)}, f32[13,48,128]{2,1,0:T(8,128)S(1)}, u32[]{:S(2)}, u32[]{:S(2)}) collective-permute-start(f32[13,48,128]{2,1,0:T(8,128)S(1)} %get-tuple-element.121), channel_id=1, source_target_pairs={{0,12},{4,0},{8,4},{12,8},{1,13},{5,1},{9,5},{13,9},{2,14},{6,2},{... | collective-permute-start | bytes 958472 | tf_op jit(solution)/shard_map/ppermute | solution.py:569
  38.6 2.0 %collective-permute-start.9 = (f32[13,24,128]{2,1,0:T(8,128)S(1)}, f32[13,24,128]{2,1,0:T(8,128)S(1)}, u32[]{:S(2)}, u32[]{:S(2)}) collective-permute-start(f32[13,24,128]{2,1,0:T(8,128)S(1)} %get-tuple-element.119), channel_id=1, source_target_pairs={{0,16},{16,0},{1,17},{17,1},{2,18},{18,2},{3,19},{19,3},{4,20},{20... | collective-permute-start | bytes 479240 | tf_op jit(solution)/shard_map/ppermute | solution.py:624
  40.6 3.8 %collective-permute-start.13 = (f32[13,8,128]{2,1,0:T(8,128)S(1)}, f32[13,8,128]{2,1,0:T(8,128)S(1)}, u32[]{:S(2)}, u32[]{:S(2)}) collective-permute-start(f32[13,8,128]{2,1,0:T(8,128)S(1)} %get-tuple-element.123), channel_id=1, source_target_pairs={{0,3},{1,0},{2,1},{3,2},{4,7},{5,4},{6,5},{7,6},{8,11},{9,8},{10,9... | collective-permute-start | bytes 159752 | tf_op jit(solution)/shard_map/ppermute | solution.py:569
  44.5 5.6 %shard_map.48 = (f32[128,128]{1,0:T(8,128)S(1)}, f32[128,128]{1,0:T(8,128)S(1)}, f32[128,128]{1,0:T(8,128)S(1)}, f32[128,128]{1,0:T(8,128)S(1)}, f32[128,128]{1,...) custom-call(f32[13,128,128]{2,1,0:T(8,128)S(1)} %get-tuple-element.1, ...), custom_call_target="tpu_custom_call" | custom-call | tf_op jit(solution)/shard_map/pallas_call | solution.py:630
  50.1 0.0 collective-permute-done.12.zlo_ref
  50.1 0.0 collective-permute-done.9.xlo_ref.xhi_ref
  50.1 0.0 collective-permute-done.10.ylo_ref
  50.1 6.2 %shard_map.49 = (f32[13,128,128]{2,1,0:T(8,128)S(1)}, f32[13,144,128]{2,1,0:T(8,128)S(1)}, f32[13,24,128]{2,1,0:T(8,128)S(1)}, f32[13,48,128]{2,1,0:T(8,128)S(1)...) custom-call(s32[5]{0:T(128)S(1)} %stack.15.place, ...), custom_call_target="tpu_custom_call" | custom-call | tf_op jit(solution)/shard_map/pallas_call | solution.py:633
  56.4 0.1 collective-permute-start.15
  56.4 1.7 %collective-permute-start.16 = (f32[13,48,128]{2,1,0:T(8,128)S(1)}, f32[13,48,128]{2,1,0:T(8,128)S(1)}, u32[]{:S(2)}, u32[]{:S(2)}) collective-permute-start(f32[13,48,128]{2,1,0:T(8,128)S(1)} %get-tuple-element.140), channel_id=1, source_target_pairs={{0,12},{4,0},{8,4},{12,8},{1,13},{5,1},{9,5},{13,9},{2,14},{6,2},{... | collective-permute-start | bytes 958472 | tf_op jit(solution)/shard_map/ppermute | solution.py:569
  58.2 0.0 collective-permute-start.17
  58.2 3.8 %collective-permute-start.18 = (f32[13,8,128]{2,1,0:T(8,128)S(1)}, f32[13,8,128]{2,1,0:T(8,128)S(1)}, u32[]{:S(2)}, u32[]{:S(2)}) collective-permute-start(f32[13,8,128]{2,1,0:T(8,128)S(1)} %get-tuple-element.142), channel_id=1, source_target_pairs={{0,3},{1,0},{2,1},{3,2},{4,7},{5,4},{6,5},{7,6},{8,11},{9,8},{10,9... | collective-permute-start | bytes 159752 | tf_op jit(solution)/shard_map/ppermute | solution.py:569
  62.0 5.6 %shard_map.50 = (f32[128,128]{1,0:T(8,128)S(1)}, f32[128,128]{1,0:T(8,128)S(1)}, f32[128,128]{1,0:T(8,128)S(1)}, f32[128,128]{1,0:T(8,128)S(1)}, f32[128,128]{1,...) custom-call(f32[13,128,128]{2,1,0:T(8,128)S(1)} %get-tuple-element.1, ...), custom_call_target="tpu_custom_call" | custom-call | tf_op jit(solution)/shard_map/pallas_call | solution.py:630
  67.6 0.0 collective-permute-done.17.zlo_ref
  67.7 0.0 copy-start
  67.7 6.2 %shard_map.51.third_ref = f32[13,128,128]{2,1,0:T(8,128)S(1)} custom-call(s32[5]{0:T(128)S(1)} %stack.15.place, f32[13,128,128]{2,1,0:T(8,128)S(1)} %get-tuple-element.136.u_ref, f32[13,144,128]{2,1,0:T(8,128)S(1)} %get-tuple-element.137.uz_ref, f32[13,128,128]{2,1,0:T(8,128)S(1)} %get-tuple-element.98.u_ref.start_ref, f32[13,8,128]{2,1,0:T(8,128)S(1)} %copy-done.3, ...), custom_call_target="tpu_custom_call" | custom-call | tf_op jit(solution)/shard_map/pallas_call | solution.py:633
  73.9 2.8 %shard_map.52 = f32[13,128,128]{2,1,0:T(8,128)} custom-call(f32[13,128,128]{2,1,0:T(8,128)S(1)} %shard_map.51.third_ref, s32[128,128]{1,0:T(8,128)S(1)} %bitcast.7), custom_call_target="tpu_custom_call" | custom-call | tf_op jit(solution)/shard_map/pallas_call | solution.py:641
  (19 shorter events, 0.0 us)
Async XLA Ops:
  0.8 16.4 %copy-start.1 = (f32[13,128,128]{2,1,0:T(8,128)S(1)}, f32[13,128,128]{2,1,0:T(8,128)}, u32[]{:S(2)}) copy-start(f32[13,128,128]{2,1,0:T(8,128)} %get-tuple-element.36.state_ref) | copy-start | bytes 2555908 | tf_op jit(solution)/shard_map/cond
  0.8 16.4 %copy-start.6 = (f32[13,8,128]{2,1,0:T(8,128)S(1)}, f32[13,8,128]{2,1,0:T(8,128)}, u32[]{:S(2)}) copy-start(f32[13,8,128]{2,1,0:T(8,128)} %get-tuple-element.37.fresh_ref) | copy-start | bytes 159748 | tf_op jit(solution)/shard_map/cond
  1.9 15.2 %collective-permute-start.2 = (f32[13,72,128]{2,1,0:T(8,128)S(1)}, f32[13,72,128]{2,1,0:T(8,128)S(1)}, u32[]{:S(2)}, u32[]{:S(2)}) collective-permute-start(f32[13,72,128]{2,1,0:T(8,128)S(1)} %slice.10), channel_id=1, source_target_pairs={{16,0},{17,1},{18,2},{19,3},{20,4},{21,5},{22,6},{23,7},{24,8},{25... | collective-permute-start | bytes 1437704 | tf_op jit(solution)/shard_map/cond/branch_2_fun/ppermute | solution.py:569
  18.8 11.8 %collective-permute-start.5 = (f32[13,48,128]{2,1,0:T(8,128)S(1)}, f32[13,48,128]{2,1,0:T(8,128)S(1)}, u32[]{:S(2)}, u32[]{:S(2)}) collective-permute-start(f32[13,48,128]{2,1,0:T(8,128)S(1)} %get-tuple-element.101), channel_id=1, source_target_pairs={{0,4},{4,8},{8,12},{12,0},{1,5},{5,9},{9,13},{13,1},{2,6},{6,10},{... | collective-permute-start | bytes 958472 | tf_op jit(solution)/shard_map/ppermute | solution.py:569
  18.8 11.8 %collective-permute-start.6 = (f32[13,48,128]{2,1,0:T(8,128)S(1)}, f32[13,48,128]{2,1,0:T(8,128)S(1)}, u32[]{:S(2)}, u32[]{:S(2)}) collective-permute-start(f32[13,48,128]{2,1,0:T(8,128)S(1)} %get-tuple-element.102), channel_id=1, source_target_pairs={{0,12},{4,0},{8,4},{12,8},{1,13},{5,1},{9,5},{13,9},{2,14},{6,2},{... | collective-permute-start | bytes 958472 | tf_op jit(solution)/shard_map/ppermute | solution.py:569
  20.6 10.0 %collective-permute-start.4 = (f32[13,24,128]{2,1,0:T(8,128)S(1)}, f32[13,24,128]{2,1,0:T(8,128)S(1)}, u32[]{:S(2)}, u32[]{:S(2)}) collective-permute-start(f32[13,24,128]{2,1,0:T(8,128)S(1)} %get-tuple-element.100), channel_id=1, source_target_pairs={{0,16},{16,0},{1,17},{17,1},{2,18},{18,2},{3,19},{19,3},{4,20},{20... | collective-permute-start | bytes 479240 | tf_op jit(solution)/shard_map/ppermute | solution.py:624
  20.6 10.0 %collective-permute-start.7 = (f32[13,8,128]{2,1,0:T(8,128)}, f32[13,8,128]{2,1,0:T(8,128)S(1)}, u32[]{:S(2)}, u32[]{:S(2)}) collective-permute-start(f32[13,8,128]{2,1,0:T(8,128)} %get-tuple-element.103), channel_id=1, source_target_pairs={{0,1},{1,2},{2,3},{3,0},{4,5},{5,6},{6,7},{7,4},{8,9},{9,10},{10,1... | collective-permute-start | bytes 159752 | tf_op jit(solution)/shard_map/ppermute | solution.py:569
  23.0 7.6 %collective-permute-start.8 = (f32[13,8,128]{2,1,0:T(8,128)}, f32[13,8,128]{2,1,0:T(8,128)S(1)}, u32[]{:S(2)}, u32[]{:S(2)}) collective-permute-start(f32[13,8,128]{2,1,0:T(8,128)} %get-tuple-element.104), channel_id=1, source_target_pairs={{0,3},{1,0},{2,1},{3,2},{4,7},{5,4},{6,5},{7,6},{8,11},{9,8},{10,9... | collective-permute-start | bytes 159752 | tf_op jit(solution)/shard_map/ppermute | solution.py:569
  25.0 5.6 %copy-start.3 = (f32[13,8,128]{2,1,0:T(8,128)S(1)}, f32[13,8,128]{2,1,0:T(8,128)}, u32[]{:S(2)}) copy-start(f32[13,8,128]{2,1,0:T(8,128)} %fresh_ref.5) | copy-start | bytes 159748
  36.8 13.3 %collective-permute-start.10 = (f32[13,48,128]{2,1,0:T(8,128)S(1)}, f32[13,48,128]{2,1,0:T(8,128)S(1)}, u32[]{:S(2)}, u32[]{:S(2)}) collective-permute-start(f32[13,48,128]{2,1,0:T(8,128)S(1)} %get-tuple-element.120), channel_id=1, source_target_pairs={{0,4},{4,8},{8,12},{12,0},{1,5},{5,9},{9,13},{13,1},{2,6},{6,10},{... | collective-permute-start | bytes 958472 | tf_op jit(solution)/shard_map/ppermute | solution.py:569
  36.9 13.3 %collective-permute-start.11 = (f32[13,48,128]{2,1,0:T(8,128)S(1)}, f32[13,48,128]{2,1,0:T(8,128)S(1)}, u32[]{:S(2)}, u32[]{:S(2)}) collective-permute-start(f32[13,48,128]{2,1,0:T(8,128)S(1)} %get-tuple-element.121), channel_id=1, source_target_pairs={{0,12},{4,0},{8,4},{12,8},{1,13},{5,1},{9,5},{13,9},{2,14},{6,2},{... | collective-permute-start | bytes 958472 | tf_op jit(solution)/shard_map/ppermute | solution.py:569
  38.6 11.5 %collective-permute-start.9 = (f32[13,24,128]{2,1,0:T(8,128)S(1)}, f32[13,24,128]{2,1,0:T(8,128)S(1)}, u32[]{:S(2)}, u32[]{:S(2)}) collective-permute-start(f32[13,24,128]{2,1,0:T(8,128)S(1)} %get-tuple-element.119), channel_id=1, source_target_pairs={{0,16},{16,0},{1,17},{17,1},{2,18},{18,2},{3,19},{19,3},{4,20},{20... | collective-permute-start | bytes 479240 | tf_op jit(solution)/shard_map/ppermute | solution.py:624
  40.6 9.4 %collective-permute-start.12 = (f32[13,8,128]{2,1,0:T(8,128)S(1)}, f32[13,8,128]{2,1,0:T(8,128)S(1)}, u32[]{:S(2)}, u32[]{:S(2)}) collective-permute-start(f32[13,8,128]{2,1,0:T(8,128)S(1)} %get-tuple-element.122), channel_id=1, source_target_pairs={{0,1},{1,2},{2,3},{3,0},{4,5},{5,6},{6,7},{7,4},{8,9},{9,10},{10,1... | collective-permute-start | bytes 159752 | tf_op jit(solution)/shard_map/ppermute | solution.py:569
  40.6 9.4 %collective-permute-start.13 = (f32[13,8,128]{2,1,0:T(8,128)S(1)}, f32[13,8,128]{2,1,0:T(8,128)S(1)}, u32[]{:S(2)}, u32[]{:S(2)}) collective-permute-start(f32[13,8,128]{2,1,0:T(8,128)S(1)} %get-tuple-element.123), channel_id=1, source_target_pairs={{0,3},{1,0},{2,1},{3,2},{4,7},{5,4},{6,5},{7,6},{8,11},{9,8},{10,9... | collective-permute-start | bytes 159752 | tf_op jit(solution)/shard_map/ppermute | solution.py:569
  56.4 11.3 %collective-permute-start.15 = (f32[13,48,128]{2,1,0:T(8,128)S(1)}, f32[13,48,128]{2,1,0:T(8,128)S(1)}, u32[]{:S(2)}, u32[]{:S(2)}) collective-permute-start(f32[13,48,128]{2,1,0:T(8,128)S(1)} %get-tuple-element.139), channel_id=1, source_target_pairs={{0,4},{4,8},{8,12},{12,0},{1,5},{5,9},{9,13},{13,1},{2,6},{6,10},{... | collective-permute-start | bytes 958472 | tf_op jit(solution)/shard_map/ppermute | solution.py:569
  56.4 11.2 %collective-permute-start.16 = (f32[13,48,128]{2,1,0:T(8,128)S(1)}, f32[13,48,128]{2,1,0:T(8,128)S(1)}, u32[]{:S(2)}, u32[]{:S(2)}) collective-permute-start(f32[13,48,128]{2,1,0:T(8,128)S(1)} %get-tuple-element.140), channel_id=1, source_target_pairs={{0,12},{4,0},{8,4},{12,8},{1,13},{5,1},{9,5},{13,9},{2,14},{6,2},{... | collective-permute-start | bytes 958472 | tf_op jit(solution)/shard_map/ppermute | solution.py:569
  58.2 9.5 %collective-permute-start.14 = (f32[13,24,128]{2,1,0:T(8,128)S(1)}, f32[13,24,128]{2,1,0:T(8,128)S(1)}, u32[]{:S(2)}, u32[]{:S(2)}) collective-permute-start(f32[13,24,128]{2,1,0:T(8,128)S(1)} %get-tuple-element.138), channel_id=1, source_target_pairs={{0,16},{16,0},{1,17},{17,1},{2,18},{18,2},{3,19},{19,3},{4,20},{20... | collective-permute-start | bytes 479240 | tf_op jit(solution)/shard_map/ppermute | solution.py:624
  58.2 9.4 %collective-permute-start.17 = (f32[13,8,128]{2,1,0:T(8,128)S(1)}, f32[13,8,128]{2,1,0:T(8,128)S(1)}, u32[]{:S(2)}, u32[]{:S(2)}) collective-permute-start(f32[13,8,128]{2,1,0:T(8,128)S(1)} %get-tuple-element.141), channel_id=1, source_target_pairs={{0,1},{1,2},{2,3},{3,0},{4,5},{5,6},{6,7},{7,4},{8,9},{9,10},{10,1... | collective-permute-start | bytes 159752 | tf_op jit(solution)/shard_map/ppermute | solution.py:569
  58.2 9.4 %collective-permute-start.18 = (f32[13,8,128]{2,1,0:T(8,128)S(1)}, f32[13,8,128]{2,1,0:T(8,128)S(1)}, u32[]{:S(2)}, u32[]{:S(2)}) collective-permute-start(f32[13,8,128]{2,1,0:T(8,128)S(1)} %get-tuple-element.142), channel_id=1, source_target_pairs={{0,3},{1,0},{2,1},{3,2},{4,7},{5,4},{6,5},{7,6},{8,11},{9,8},{10,9... | collective-permute-start | bytes 159752 | tf_op jit(solution)/shard_map/ppermute | solution.py:569
  67.7 6.2 %copy-start = (s32[16,8,128]{2,1,0:T(8,128)S(1)}, s32[16,8,128]{2,1,0:T(8,128)}, u32[]{:S(2)}) copy-start(s32[16,8,128]{2,1,0:T(8,128)} %param.10) | copy-start | bytes 196612
